TPU v7x, 32 devices: a whole 2x2x4 slice. The times are simulated.
32 devices in a mesh: seq: 8 (over z, y), dp: 4 (over x, core).
Axes of the slice: x: 2, y: 2, z: 4, core: 2. Of those that a mesh axis runs over, the one named last changes fastest.
Arguments:
- signal: bfloat16 [4, 8192, 384], P('dp', 'seq'), may hold values from -6 to 6
- filter_raw: bfloat16 [8192, 384], P('seq'), may hold values from -6 to 6
- cotangent: bfloat16 [4, 8192, 384], P('dp', 'seq'), may hold values from -6 to 6
- block_mask: int32 [4, 8], P('dp', 'seq'), may hold values from 0 to 1, as said below
Outputs:
- conv_out: bfloat16 [4, 8192, 384], P('dp', 'seq')
- signal_grad: bfloat16 [4, 8192, 384], P('dp', 'seq')
- filter_grad: bfloat16 [8192, 384], P('seq')
Inputs may be any that keep to these rules, and one draw needn't show every extreme that they name: `block_mask`: each sequence's row is 1 on a leading run of blocks and 0 on the rest; every row has both.
All inputs are finite; a program needn't handle non-finite values.
Results may differ from a plain program's by a relative error of at most 0.013.
Values may be sent and summed in bfloat16 or wider, within the bound.
No kernel may reach another device: no remote copies, remote signals or barrier semaphores. Data moves between devices by JAX's collectives and lax.ppermute only.
A program may use at most 128 MiB of HBM per device.

v0:
```python
import math

import jax
import jax.numpy as jnp
from jax import lax
from jax.sharding import PartitionSpec as P

BLK = 1024
RAD = 32


def angle_table(row_ids, col_ids, period):
    product = row_ids[:, None] * col_ids[None, :] % period
    return 2.0 * math.pi / period * product.astype(jnp.float32)


def per_device(signal, filter_raw, cotangent, block_mask):
    tokens = filter_raw.shape[0]
    channels = filter_raw.shape[1]
    seq_count = lax.axis_size("seq")
    seq_index = lax.axis_index("seq")
    local_blocks = tokens // BLK
    real_blocks = local_blocks * seq_count
    all_blocks = 2 * real_blocks
    column_width = BLK // seq_count
    freq_width = all_blocks // seq_count
    period = all_blocks * BLK
    freq_ids = jnp.arange(all_blocks, dtype=jnp.int32)
    block_ids = jnp.arange(real_blocks, dtype=jnp.int32)
    radix_ids = jnp.arange(RAD, dtype=jnp.int32)
    outer_angle = angle_table(freq_ids, block_ids, all_blocks)
    cos_one = jnp.cos(outer_angle).astype(jnp.bfloat16)
    sin_one = jnp.sin(outer_angle).astype(jnp.bfloat16)
    radix_angle = angle_table(radix_ids, radix_ids, RAD)
    cos_rad = jnp.cos(radix_angle).astype(jnp.bfloat16)
    sin_rad = jnp.sin(radix_angle).astype(jnp.bfloat16)
    inner_angle = angle_table(radix_ids, radix_ids, BLK)
    inner_cos = jnp.cos(inner_angle)[None, :, :, None]
    inner_sin = jnp.sin(inner_angle)[None, :, :, None]
    column_ids = seq_index * column_width + jnp.arange(column_width, dtype=jnp.int32)
    column_angle = angle_table(freq_ids, column_ids, period)
    column_cos = jnp.cos(column_angle)[:, :, None]
    column_sin = jnp.sin(column_angle)[:, :, None]
    own_freqs = seq_index * freq_width + jnp.arange(freq_width, dtype=jnp.int32)
    freq_angle = angle_table(own_freqs, jnp.arange(BLK, dtype=jnp.int32), period)
    freq_cos = jnp.cos(freq_angle)[:, :, None]
    freq_sin = jnp.sin(freq_angle)[:, :, None]
    factor = 1.0 / (all_blocks * BLK * math.sqrt(real_blocks * BLK))

    def outer_section(portion):
        first_real = jnp.einsum("ka,abc->kbc", cos_one, portion, preferred_element_type=jnp.float32)
        first_imag = -jnp.einsum(
            "ka,abc->kbc", sin_one, portion, preferred_element_type=jnp.float32
        )
        turned_real = first_real * column_cos + first_imag * column_sin
        turned_imag = first_imag * column_cos - first_real * column_sin
        return jnp.stack([turned_real, turned_imag]).astype(jnp.bfloat16)

    def inner_section(portion):
        rows_here = portion.shape[1]
        width = portion.shape[3]
        parted = portion.reshape(2, rows_here, RAD, RAD, width)
        mid_real = jnp.einsum(
            "pr,kpqc->krqc", cos_rad, parted[0], preferred_element_type=jnp.float32
        ) + jnp.einsum("pr,kpqc->krqc", sin_rad, parted[1], preferred_element_type=jnp.float32)
        mid_imag = jnp.einsum(
            "pr,kpqc->krqc", cos_rad, parted[1], preferred_element_type=jnp.float32
        ) - jnp.einsum("pr,kpqc->krqc", sin_rad, parted[0], preferred_element_type=jnp.float32)
        spun_real = (mid_real * inner_cos + mid_imag * inner_sin).astype(jnp.bfloat16)
        spun_imag = (mid_imag * inner_cos - mid_real * inner_sin).astype(jnp.bfloat16)
        last_real = jnp.einsum(
            "qs,krqc->ksrc", cos_rad, spun_real, preferred_element_type=jnp.float32
        ) + jnp.einsum("qs,krqc->ksrc", sin_rad, spun_imag, preferred_element_type=jnp.float32)
        last_imag = jnp.einsum(
            "qs,krqc->ksrc", cos_rad, spun_imag, preferred_element_type=jnp.float32
        ) - jnp.einsum("qs,krqc->ksrc", sin_rad, spun_real, preferred_element_type=jnp.float32)
        return jnp.stack([last_real, last_imag]).reshape(2, rows_here, BLK, width)

    def forward(values):
        spread = outer_section(
            lax.all_to_all(values, "seq", split_axis=1, concat_axis=0, tiled=True)
        )
        return inner_section(lax.all_to_all(spread, "seq", split_axis=1, concat_axis=2, tiled=True))

    def outer_back(portion):
        combined = jnp.einsum(
            "ka,kbc->abc", cos_one, portion[0], preferred_element_type=jnp.float32
        ) - jnp.einsum("ka,kbc->abc", sin_one, portion[1], preferred_element_type=jnp.float32)
        return (combined * factor).astype(jnp.bfloat16)

    def inverse(spectrum):
        width = spectrum.shape[3]
        rounded_spec = spectrum.astype(jnp.bfloat16).reshape(2, freq_width, RAD, RAD, width)
        mid_real = jnp.einsum(
            "sq,ksrc->krqc", cos_rad, rounded_spec[0], preferred_element_type=jnp.float32
        ) - jnp.einsum(
            "sq,ksrc->krqc", sin_rad, rounded_spec[1], preferred_element_type=jnp.float32
        )
        mid_imag = jnp.einsum(
            "sq,ksrc->krqc", cos_rad, rounded_spec[1], preferred_element_type=jnp.float32
        ) + jnp.einsum(
            "sq,ksrc->krqc", sin_rad, rounded_spec[0], preferred_element_type=jnp.float32
        )
        spun_real = (mid_real * inner_cos - mid_imag * inner_sin).astype(jnp.bfloat16)
        spun_imag = (mid_imag * inner_cos + mid_real * inner_sin).astype(jnp.bfloat16)
        back_real = jnp.einsum(
            "rp,krqc->kpqc", cos_rad, spun_real, preferred_element_type=jnp.float32
        ) - jnp.einsum("rp,krqc->kpqc", sin_rad, spun_imag, preferred_element_type=jnp.float32)
        back_imag = jnp.einsum(
            "rp,krqc->kpqc", cos_rad, spun_imag, preferred_element_type=jnp.float32
        ) + jnp.einsum("rp,krqc->kpqc", sin_rad, spun_real, preferred_element_type=jnp.float32)
        back_real = back_real.reshape(freq_width, BLK, width)
        back_imag = back_imag.reshape(freq_width, BLK, width)
        turned_real = back_real * freq_cos - back_imag * freq_sin
        turned_imag = back_imag * freq_cos + back_real * freq_sin
        packed = jnp.stack([turned_real, turned_imag]).astype(jnp.bfloat16)
        columns = outer_back(lax.all_to_all(packed, "seq", split_axis=2, concat_axis=1, tiled=True))
        return lax.all_to_all(columns, "seq", split_axis=0, concat_axis=1, tiled=True)

    mask_blocks = block_mask[0].astype(jnp.bfloat16)[:, None, None]
    masked = signal[0].reshape(local_blocks, BLK, channels) * mask_blocks
    grad_input = cotangent[0].reshape(local_blocks, BLK, channels)
    filter_input = filter_raw.reshape(local_blocks, BLK, channels)
    spec_signal = forward(masked)
    spec_grad = forward(grad_input)
    spec_filter = forward(filter_input)
    signal_real, signal_imag = (spec_signal[0], spec_signal[1])
    filter_real, filter_imag = (spec_filter[0], spec_filter[1])
    grad_real, grad_imag = (spec_grad[0], spec_grad[1])
    spec_out = jnp.stack(
        [
            signal_real * filter_real - signal_imag * filter_imag,
            signal_real * filter_imag + signal_imag * filter_real,
        ]
    )
    spec_input = jnp.stack(
        [
            grad_real * filter_real + grad_imag * filter_imag,
            grad_imag * filter_real - grad_real * filter_imag,
        ]
    )
    spec_weight = jnp.stack(
        [
            grad_real * signal_real + grad_imag * signal_imag,
            grad_imag * signal_real - grad_real * signal_imag,
        ]
    )
    weight_total = lax.psum(spec_weight.astype(jnp.bfloat16), "dp").astype(jnp.float32)
    conv_rows = inverse(spec_out)
    input_rows = inverse(spec_input)
    weight_rows = inverse(weight_total)
    input_rows = input_rows * mask_blocks
    return (conv_rows, input_rows, weight_rows.reshape(tokens, channels))


def solution(mesh):
    placed = (P("dp", "seq", None), P("seq", None), P("dp", "seq", None), P("dp", "seq"))
    return jax.shard_map(
        per_device,
        mesh=mesh,
        in_specs=placed,
        out_specs=(P("dp", "seq", None), P("dp", "seq", None), P("seq", None)),
        check_vma=False,
    )
```

profile of v0, /device:TPU:0, one launch (start us, length us, event | category | flops | bytes accessed | tf_op | source)
XLA Modules:
  0.0 810.2 jit_solution(1508061687473184049)
XLA Ops:
  10.0 5.4 reduce
  16.6 7.8 all-to-all-start.6
  25.6 5.4 reduce.1
  32.1 12.4 %all-to-all-done.6 = bf16[8,2,24576]{2,1,0:T(2,128)(2,1)S(1)} async-done(((bf16[8,2,24576]{2,1,0:T(2,128)(2,1)}), bf16[8,2,24576]{2,1,0:T(2,128)(2,1)S(1)}, u32[]{:S(2)}, u32[]{:S(2)}) %all-to-all-start.6) | async-done | bytes 786464 | tf_op jit(solution)/shard_map/all_to_all | solution.py:81
  51.6 5.4 reduce.2
  58.1 11.0 %all-to-all-done.2 = bf16[8,2,24576]{2,1,0:T(2,128)(2,1)} async-done(((bf16[8,2,24576]{2,1,0:T(2,128)(2,1)}), bf16[8,2,24576]{2,1,0:T(2,128)(2,1)}, u32[]{:S(2)}, u32[]{:S(2)}) %all-to-all-start.2) | async-done | bytes 786464 | tf_op jit(solution)/shard_map/all_to_all | solution.py:81
  93.3 5.5 reshape.685
  102.6 6.5 fusion.20
  120.1 66.1 %all-to-all-done.1 = bf16[2,16,128,384]{3,2,0,1:T(8,128)(2,1)S(1)} async-done(((bf16[2,16,128,384]{3,2,0,1:T(8,128)(2,1)}), bf16[2,16,128,384]{3,2,0,1:T(8,128)(2,1)S(1)}, u32[]{:S(2)}, u32[]{:S(2)}) %all-to-all-start.1) | async-done | bytes 3145760 | tf_op jit(solution)/shard_map/all_to_all | solution.py:83
  197.0 65.6 %all-to-all-done.3 = bf16[2,16,128,384]{3,2,0,1:T(8,128)(2,1)} async-done(((bf16[2,16,128,384]{3,2,0,1:T(8,128)(2,1)}), bf16[2,16,128,384]{3,2,0,1:T(8,128)(2,1)}, u32[]{:S(2)}, u32[]{:S(2)}) %all-to-all-start.3) | async-done | bytes 3145760 | tf_op jit(solution)/shard_map/all_to_all | solution.py:83
  286.1 51.0 %all-to-all-done.7 = bf16[2,16,128,384]{3,2,0,1:T(8,128)(2,1)S(1)} async-done(((bf16[2,16,128,384]{3,2,0,1:T(8,128)(2,1)}), bf16[2,16,128,384]{3,2,0,1:T(8,128)(2,1)S(1)}, u32[]{:S(2)}, u32[]{:S(2)}) %all-to-all-start.7) | async-done | bytes 3145760 | tf_op jit(solution)/shard_map/all_to_all | solution.py:83
  343.7 6.8 fusion.3
  361.9 5.6 fusion.26
  390.3 55.4 %all-reduce.2.cloned.1.call-done = bf16[2,2,1024,384]{3,2,1,0:T(8,128)(2,1)} async-done(((bf16[2,2,1024,384]{3,2,1,0:T(8,128)(2,1)}), bf16[2,2,1024,384]{3,2,1,0:T(8,128)(2,1)}) %all-reduce.2.cloned.1.call-update) | async-done | bytes 3145744 | tf_op jit(solution)/shard_map/psum | solution.py:148
  455.8 6.6 fusion.29
  487.9 4.9 copy.346
  492.8 5.5 all-to-all-start.10
  505.4 63.5 %all-to-all-done.10 = bf16[2,2,1024,384]{3,1,0,2:T(2,128)(2,1)S(1)} async-done(((bf16[2,2,1024,384]{3,1,0,2:T(2,128)(2,1)}), bf16[2,2,1024,384]{3,1,0,2:T(2,128)(2,1)S(1)}, u32[]{:S(2)}, u32[]{:S(2)}) %all-to-all-start.10) | async-done | bytes 3145760 | tf_op jit(solution)/shard_map/all_to_all | solution.py:117
  576.6 4.9 copy.303
  581.5 63.7 %all-to-all-done.8 = bf16[2,2,1024,384]{3,1,0,2:T(2,128)(2,1)S(1)} async-done(((bf16[2,2,1024,384]{3,1,0,2:T(2,128)(2,1)}), bf16[2,2,1024,384]{3,1,0,2:T(2,128)(2,1)S(1)}, u32[]{:S(2)}, u32[]{:S(2)}) %all-to-all-start.8) | async-done | bytes 3145760 | tf_op jit(solution)/shard_map/all_to_all | solution.py:117
  673.5 46.5 %all-to-all-done.4 = bf16[2,2,1024,384]{3,1,0,2:T(2,128)(2,1)} async-done(((bf16[2,2,1024,384]{3,1,0,2:T(2,128)(2,1)}), bf16[2,2,1024,384]{3,1,0,2:T(2,128)(2,1)}, u32[]{:S(2)}, u32[]{:S(2)}) %all-to-all-start.4) | async-done | bytes 3145760 | tf_op jit(solution)/shard_map/all_to_all | solution.py:117
  748.1 6.3 all-to-all-start.5
  766.2 7.6 all-to-all-done.5
  777.4 20.3 %all-to-all-done.9 = bf16[8,128,384]{2,1,0:T(8,128)(2,1)S(1)} async-done(((bf16[8,128,384]{2,1,0:T(8,128)(2,1)}), bf16[8,128,384]{2,1,0:T(8,128)(2,1)S(1)}, u32[]{:S(2)}, u32[]{:S(2)}) %all-to-all-start.9) | async-done | bytes 786464 | tf_op jit(solution)/shard_map/all_to_all | solution.py:118
  (189 shorter events, 254.4 us)
Async XLA Ops:
  16.6 7.8 copy-start.20
  16.6 27.9 %all-to-all-start.6 = ((bf16[8,2,24576]{2,1,0:T(2,128)(2,1)}), bf16[8,2,24576]{2,1,0:T(2,128)(2,1)S(1)}, u32[]{:S(2)}, u32[]{:S(2)}) async-start(bf16[8,2,24576]{2,1,0:T(2,128)(2,1)} %reshape.688), calls=%async_computation.6 | async-start | bytes 1572864 | tf_op jit(solution)/shard_map/all_to_all | solution.py:81
  32.1 17.8 %copy-start.19 = (bf16[1,1024,384]{2,1,0:T(8,128)(2,1)S(1)}, bf16[1,1024,384]{2,1,0:T(8,128)(2,1)}, u32[]{:S(2)}) copy-start(bf16[1,1024,384]{2,1,0:T(8,128)(2,1)} %param.4) | copy-start | bytes 2359300
  44.5 24.7 %all-to-all-start.2 = ((bf16[8,2,24576]{2,1,0:T(2,128)(2,1)}), bf16[8,2,24576]{2,1,0:T(2,128)(2,1)}, u32[]{:S(2)}, u32[]{:S(2)}) async-start(bf16[8,2,24576]{2,1,0:T(2,128)(2,1)} %reshape.686), calls=%async_computation.2 | async-start | bytes 1572864 | tf_op jit(solution)/shard_map/all_to_all | solution.py:81
  69.1 24.2 %all-to-all-start = ((bf16[8,2,24576]{2,1,0:T(2,128)(2,1)}), bf16[8,2,24576]{2,1,0:T(2,128)(2,1)}, u32[]{:S(2)}, u32[]{:S(2)}) async-start(bf16[8,2,24576]{2,1,0:T(2,128)(2,1)} %reshape.684), calls=%async_computation | async-start | bytes 1572864 | tf_op jit(solution)/shard_map/all_to_all | solution.py:81
  98.8 2.4 copy-start.9
  111.8 74.4 %all-to-all-start.1 = ((bf16[2,16,128,384]{3,2,0,1:T(8,128)(2,1)}), bf16[2,16,128,384]{3,2,0,1:T(8,128)(2,1)S(1)}, u32[]{:S(2)}, u32[]{:S(2)}) async-start(bf16[2,16,128,384]{3,2,0,1:T(8,128)(2,1)} %copy.268), calls=%async_computation.1 | async-start | bytes 6291456 | tf_op jit(solution)/shard_map/all_to_all | solution.py:83
  187.9 74.6 %all-to-all-start.3 = ((bf16[2,16,128,384]{3,2,0,1:T(8,128)(2,1)}), bf16[2,16,128,384]{3,2,0,1:T(8,128)(2,1)}, u32[]{:S(2)}, u32[]{:S(2)}) async-start(bf16[2,16,128,384]{3,2,0,1:T(8,128)(2,1)} %copy.281), calls=%async_computation.3 | async-start | bytes 6291456 | tf_op jit(solution)/shard_map/all_to_all | solution.py:83
  262.6 74.5 %all-to-all-start.7 = ((bf16[2,16,128,384]{3,2,0,1:T(8,128)(2,1)}), bf16[2,16,128,384]{3,2,0,1:T(8,128)(2,1)S(1)}, u32[]{:S(2)}, u32[]{:S(2)}) async-start(bf16[2,16,128,384]{3,2,0,1:T(8,128)(2,1)} %copy.311), calls=%async_computation.7 | async-start | bytes 6291456 | tf_op jit(solution)/shard_map/all_to_all | solution.py:83
  266.2 179.4 %all-reduce.2.cloned.1.call-start = ((), (), s32[]{:S(2)}) async-start(), calls=%async_computation.12 | async-start | bytes 6291456 | tf_op jit(solution)/shard_map/psum | solution.py:148
  339.7 4.0 copy-start.14
  367.6 2.7 copy-start
  367.6 2.7 copy-start.2
  378.0 3.5 copy-start.12
  381.5 3.8 copy-start.11
  385.3 2.6 copy-start.10
  451.8 2.5 copy-start.4
  451.8 4.0 copy-start.6
  492.8 76.1 %all-to-all-start.10 = ((bf16[2,2,1024,384]{3,1,0,2:T(2,128)(2,1)}), bf16[2,2,1024,384]{3,1,0,2:T(2,128)(2,1)S(1)}, u32[]{:S(2)}, u32[]{:S(2)}) async-start(bf16[2,2,1024,384]{3,1,0,2:T(2,128)(2,1)} %copy.346), calls=%async_computation.10 | async-start | bytes 6291456 | tf_op jit(solution)/shard_map/all_to_all | solution.py:117
  570.7 74.5 %all-to-all-start.8 = ((bf16[2,2,1024,384]{3,1,0,2:T(2,128)(2,1)}), bf16[2,2,1024,384]{3,1,0,2:T(2,128)(2,1)S(1)}, u32[]{:S(2)}, u32[]{:S(2)}) async-start(bf16[2,2,1024,384]{3,1,0,2:T(2,128)(2,1)} %copy.329), calls=%async_computation.8 | async-start | bytes 6291456 | tf_op jit(solution)/shard_map/all_to_all | solution.py:117
  645.2 74.9 %all-to-all-start.4 = ((bf16[2,2,1024,384]{3,1,0,2:T(2,128)(2,1)}), bf16[2,2,1024,384]{3,1,0,2:T(2,128)(2,1)}, u32[]{:S(2)}, u32[]{:S(2)}) async-start(bf16[2,2,1024,384]{3,1,0,2:T(2,128)(2,1)} %copy.303), calls=%async_computation.4 | async-start | bytes 6291456 | tf_op jit(solution)/shard_map/all_to_all | solution.py:117
  720.0 28.1 %all-to-all-start.11 = ((bf16[8,128,384]{2,1,0:T(8,128)(2,1)}), bf16[8,128,384]{2,1,0:T(8,128)(2,1)}, u32[]{:S(2)}, u32[]{:S(2)}) async-start(bf16[8,128,384]{2,1,0:T(8,128)(2,1)} %copy.350), calls=%async_computation.11 | async-start | bytes 1572864 | tf_op jit(solution)/shard_map/all_to_all | solution.py:118
  748.1 25.7 %all-to-all-start.5 = ((bf16[8,128,384]{2,1,0:T(8,128)(2,1)}), bf16[8,128,384]{2,1,0:T(8,128)(2,1)}, u32[]{:S(2)}, u32[]{:S(2)}) async-start(bf16[8,128,384]{2,1,0:T(8,128)(2,1)} %copy.307), calls=%async_computation.5 | async-start | bytes 1572864 | tf_op jit(solution)/shard_map/all_to_all | solution.py:118
  773.8 23.9 %all-to-all-start.9 = ((bf16[8,128,384]{2,1,0:T(8,128)(2,1)}), bf16[8,128,384]{2,1,0:T(8,128)(2,1)S(1)}, u32[]{:S(2)}, u32[]{:S(2)}) async-start(bf16[8,128,384]{2,1,0:T(8,128)(2,1)} %copy.333), calls=%async_computation.9 | async-start | bytes 1572864 | tf_op jit(solution)/shard_map/all_to_all | solution.py:118
  (10 other events, 19.0 us)
Sparse Core Ops, SparseCore 0:
  378.2 67.4 all-reduce.1
where the time goes:
time: 817 us; the launch traced here: 810 us
  waiting for transfers between devices  468 us (57%)
  local copies, waits for them, and re-layouts  134 us (16%)
  matrix products  99.5 us (12%)
  starting transfers between devices  57.1 us (7%)
  other arithmetic  35.5 us (4%)
  between operations  15.9 us (2%)
    all_to_all x3, waiting for transfers between devices, forward(): lax.all_to_all(spread, 'seq', split_axis=1, concat_axis=2, tiled=True)  183 us
    all_to_all x3, waiting for transfers between devices, inverse(): lax.all_to_all(packed, 'seq', split_axis=2, concat_axis=1, tiled=True)  174 us
    psum x1, waiting for transfers between devices, per_device(): lax.psum(spec_weight.astype(jnp.bfloat16), 'dp').astype(jnp.float32)  55.4 us
    unnamed x55, local copies, waits for them, and re-layouts  36.4 us
    all_to_all x3, waiting for transfers between devices, inverse(): lax.all_to_all(columns, 'seq', split_axis=0, concat_axis=1, tiled=True)  28 us
    all_to_all x3, waiting for transfers between devices, forward(): lax.all_to_all(values, 'seq', split_axis=1, concat_axis=0, tiled=True)  27.9 us
    unnamed x4, other arithmetic  17.9 us
    all_to_all x3, starting transfers between devices, forward(): lax.all_to_all(values, 'seq', split_axis=1, concat_axis=0, tiled=True)  17 us
  transfers between devices with their start and end apart: 13, of which 12 were waited for; matrix products, arithmetic and copies ran while one was open for 17% of the time, Pallas kernels for 0%

commit v1 on v0

v1 whole, which is shorter than its diff:
```python
import functools
import math

import jax
import jax.numpy as jnp
import ml_dtypes
import numpy as np
from jax import lax
from jax.experimental import pallas as pl
from jax.experimental.pallas import tpu as pltpu
from jax.sharding import PartitionSpec as P

LANES = 128
BLK = 1024
BF16 = ml_dtypes.bfloat16


def wave(product, period):
    angle = 2.0 * np.pi / period * (product % period)
    return np.cos(angle), np.sin(angle)


def make_tables(blocks, rows, replicas):
    coarse = blocks * rows
    freq = np.arange(coarse)
    lane = np.arange(LANES)
    own = rows // replicas
    half = rows // 2
    grid_j, grid_r = np.meshgrid(np.arange(blocks), np.arange(rows), indexing="ij")
    plain = grid_j * rows + grid_r
    cos_a, sin_a = wave((4 * freq[:, None] + 1) * np.arange(coarse)[None, :], 4 * coarse)
    first = np.zeros((2, 2, coarse, blocks, 2, rows))
    last = np.zeros((blocks, 2, rows, 2, 2, coarse))
    for which in range(2):
        first[which, 0, :, :, which, :] = cos_a[:, plain]
        first[which, 1, :, :, which, :] = -sin_a[:, plain]
        last[:, which, :, which, 0, :] = np.moveaxis(cos_a[:, plain], 0, 2)
        last[:, which, :, which, 1, :] = -np.moveaxis(sin_a[:, plain], 0, 2)
    taps = (
        np.arange(own)[:, None, None]
        + own * np.arange(replicas)[None, :, None]
        + rows * np.arange(blocks)[None, None, :]
    ).reshape(-1)
    first_taps = np.concatenate([cos_a[:, taps], -sin_a[:, taps]], axis=0)
    back = (
        np.arange(half)[:, None, None]
        + half * np.arange(2)[None, :, None]
        + rows * np.arange(blocks)[None, None, :]
    ).reshape(-1)
    last_taps = np.concatenate([cos_a[:, back], -sin_a[:, back]], axis=0).T
    twist_cos, twist_sin = wave((4 * freq[:, None] + 1) * lane[None, :], 4 * LANES * coarse)
    cos_l, sin_l = wave(lane[:, None] * lane[None, :], LANES)
    inner = np.block([[cos_l, -sin_l], [sin_l, cos_l]])
    inner_back = np.block([[cos_l, sin_l], [-sin_l, cos_l]])
    narrow = (
        first.reshape(4 * coarse, 2 * coarse),
        first_taps,
        inner,
        inner_back,
        last.reshape(2 * coarse, 4 * coarse),
        last_taps,
    )
    return tuple(t.astype(np.float32).astype(BF16) for t in narrow) + (
        twist_cos.astype(np.float32),
        twist_sin.astype(np.float32),
    )


def pack_kernel(own, group, count, mask_ref, signal_ref, grad_ref, filter_ref, send_ref, pair_scr, tap_scr):
    tokens, channels = filter_ref.shape
    rows = tokens // LANES
    pair = 2 * rows
    block_rows = BLK // LANES
    if group * count != channels:
        pair_scr[...] = jnp.zeros_like(pair_scr)
        tap_scr[...] = jnp.zeros_like(tap_scr)
    for row in range(rows):
        span = pl.ds(row * LANES, LANES)
        keep = mask_ref[0, row // block_rows].astype(jnp.float32)
        pair_scr[pl.ds(row, channels, stride=pair), :] = (
            signal_ref[0, span, :].astype(jnp.float32).T * keep
        )
        pair_scr[pl.ds(rows + row, channels, stride=pair), :] = (
            grad_ref[0, span, :].astype(jnp.float32).T
        )
    start = lax.axis_index("dp") * (own * LANES)
    for row in range(own):
        span = pl.ds(pl.multiple_of(start + row * LANES, LANES), LANES)
        tap_scr[pl.ds(row, channels, stride=own), :] = filter_ref[span, :].astype(jnp.float32).T
    for target in range(count):
        send_ref[target, : group * pair, :] = pair_scr[
            target * group * pair : (target + 1) * group * pair, :
        ].astype(jnp.bfloat16)
        send_ref[target, group * pair :, :] = tap_scr[
            target * group * own : (target + 1) * group * own, :
        ].astype(jnp.bfloat16)


def spectral_kernel(
    blocks, rows, replicas, group, factor,
    recv_ref, first_ref, first_taps_ref, inner_ref, inner_back_ref, last_ref, last_taps_ref,
    twist_cos_ref, twist_sin_ref, send_ref, tap_scr, back_scr,
):
    coarse = blocks * rows
    count = blocks * replicas
    pair = 2 * rows
    own = rows // replicas
    half = rows // 2
    tap_rows = group * own
    back_rows = group * half
    for source in range(count):
        tap_scr[source * tap_rows : (source + 1) * tap_rows, :] = recv_ref[
            source, group * pair :, :
        ].astype(jnp.float32)

    def dot(left, right):
        return jnp.dot(left, right, preferred_element_type=jnp.float32)

    def channel(index, carry):
        offset = pl.multiple_of(index * pair, pair)
        twist_cos = twist_cos_ref[...]
        twist_sin = twist_sin_ref[...]

        def turn(real, imag):
            return jnp.concatenate(
                [real * twist_cos + imag * twist_sin, imag * twist_cos - real * twist_sin], axis=1
            ).astype(jnp.bfloat16)

        taps = jnp.concatenate(
            [tap_scr[pl.ds(index * own + row, count, stride=tap_rows), :] for row in range(own)],
            axis=0,
        ).astype(jnp.bfloat16)
        spread_taps = dot(first_taps_ref[...], taps)
        data = jnp.concatenate(
            [
                recv_ref[seq * blocks : (seq + 1) * blocks, pl.ds(offset, pair), :].reshape(
                    blocks * pair, LANES
                )
                for seq in range(replicas)
            ],
            axis=1,
        )
        spread = dot(first_ref[...], data)
        turned = [turn(spread_taps[:coarse], spread_taps[coarse:])]
        for seq in range(replicas):
            part = spread[:, seq * LANES : (seq + 1) * LANES]
            for which in range(2):
                base = 2 * which * coarse
                turned.append(
                    turn(part[base : base + coarse], part[base + coarse : base + 2 * coarse])
                )
        spectrum = dot(jnp.concatenate(turned, axis=0), inner_ref[...])

        def pick(place):
            piece = spectrum[place * coarse : (place + 1) * coarse]
            return piece[:, :LANES], piece[:, LANES:]

        filter_real, filter_imag = pick(0)
        products = []
        weight_real = weight_imag = None
        for seq in range(replicas):
            signal_real, signal_imag = pick(1 + 2 * seq)
            grad_real, grad_imag = pick(2 + 2 * seq)
            out = (
                signal_real * filter_real - signal_imag * filter_imag,
                signal_real * filter_imag + signal_imag * filter_real,
            )
            into = (
                grad_real * filter_real + grad_imag * filter_imag,
                grad_imag * filter_real - grad_real * filter_imag,
            )
            term_real = grad_real * signal_real + grad_imag * signal_imag
            term_imag = grad_imag * signal_real - grad_real * signal_imag
            weight_real = term_real if weight_real is None else weight_real + term_real
            weight_imag = term_imag if weight_imag is None else weight_imag + term_imag
            products.append(jnp.concatenate(out, axis=1).astype(jnp.bfloat16))
            products.append(jnp.concatenate(into, axis=1).astype(jnp.bfloat16))
        products.append(
            jnp.concatenate([weight_real, weight_imag], axis=1).astype(jnp.bfloat16)
        )
        inverted = dot(jnp.concatenate(products, axis=0), inner_back_ref[...])

        def turn_back(place):
            piece = inverted[place * coarse : (place + 1) * coarse]
            real, imag = piece[:, :LANES], piece[:, LANES:]
            return jnp.concatenate(
                [real * twist_cos - imag * twist_sin, imag * twist_cos + real * twist_sin], axis=0
            ).astype(jnp.bfloat16)

        columns = jnp.concatenate(
            [
                jnp.concatenate([turn_back(2 * seq), turn_back(2 * seq + 1)], axis=0)
                for seq in range(replicas)
            ],
            axis=1,
        )
        result = (dot(last_ref[...], columns) * factor).astype(jnp.bfloat16)
        for seq in range(replicas):
            send_ref[seq * blocks : (seq + 1) * blocks, pl.ds(offset, pair), :] = result[
                :, seq * LANES : (seq + 1) * LANES
            ].reshape(blocks, pair, LANES)
        weights = dot(last_taps_ref[...], turn_back(2 * replicas)) * factor
        for row in range(half):
            back_scr[pl.ds(index * half + row, 2 * blocks, stride=back_rows), :] = weights[
                row * 2 * blocks : (row + 1) * 2 * blocks
            ]
        return carry

    lax.fori_loop(0, group, channel, 0)
    for target in range(count):
        place = (target // blocks) % 2 * blocks + target % blocks
        send_ref[target, group * pair :, :] = back_scr[
            place * back_rows : (place + 1) * back_rows, :
        ].astype(jnp.bfloat16)


def unpack_kernel(group, mask_ref, recv_ref, conv_ref, grad_ref, pair_scr):
    tokens, channels = conv_ref.shape[1:]
    rows = tokens // LANES
    pair = 2 * rows
    block_rows = BLK // LANES
    size = group * pair
    for source in range(recv_ref.shape[0]):
        pair_scr[source * size : (source + 1) * size, :] = recv_ref[source, :size, :].astype(
            jnp.float32
        )
    for row in range(rows):
        span = pl.ds(row * LANES, LANES)
        keep = mask_ref[0, row // block_rows].astype(jnp.float32)
        conv_ref[0, span, :] = pair_scr[pl.ds(row, channels, stride=pair), :].T.astype(jnp.bfloat16)
        grad_ref[0, span, :] = (
            pair_scr[pl.ds(rows + row, channels, stride=pair), :].T * keep
        ).astype(jnp.bfloat16)


def unpack_taps_kernel(group, own_ref, other_ref, taps_ref, scr):
    tokens, channels = taps_ref.shape
    half = tokens // LANES // 2
    size = group * half
    side = lax.rem(lax.axis_index("dp"), 2)
    for place, ref in enumerate((own_ref, other_ref)):
        for source in range(ref.shape[0]):
            scr[source * size : (source + 1) * size, :] = ref[source].astype(jnp.float32)
        start = jnp.where(side == place, 0, half * LANES)
        for row in range(half):
            span = pl.ds(pl.multiple_of(start + row * LANES, LANES), LANES)
            taps_ref[span, :] = scr[pl.ds(row, channels, stride=half), :].T.astype(jnp.bfloat16)


VMEM = pl.BlockSpec(memory_space=pltpu.VMEM)
SMEM = pl.BlockSpec(memory_space=pltpu.SMEM)
LIMIT = pltpu.CompilerParams(vmem_limit_bytes=48 * 1024 * 1024)


def per_device(signal, filter_raw, cotangent, block_mask):
    tokens, channels = filter_raw.shape
    blocks = lax.axis_size("seq")
    replicas = lax.axis_size("dp")
    count = blocks * replicas
    group = -(-channels // count)
    rows = tokens // LANES
    pair = 2 * rows
    own = rows // replicas
    half = rows // 2
    total = tokens * blocks
    coarse = total // LANES
    factor = 1.0 / (total * math.sqrt(total))
    everyone = ("dp", "seq")
    tables = [jnp.asarray(t) for t in make_tables(blocks, rows, replicas)]

    packed = pl.pallas_call(
        functools.partial(pack_kernel, own, group, count),
        out_shape=jax.ShapeDtypeStruct((count, group * (pair + own), LANES), jnp.bfloat16),
        in_specs=[SMEM, VMEM, VMEM, VMEM],
        out_specs=VMEM,
        scratch_shapes=[
            pltpu.VMEM((count * group * pair, LANES), jnp.float32),
            pltpu.VMEM((count * group * own, LANES), jnp.float32),
        ],
        compiler_params=LIMIT,
        name="pack",
    )(block_mask, signal, cotangent, filter_raw)
    received = lax.all_to_all(packed, everyone, split_axis=0, concat_axis=0, tiled=True)
    results = pl.pallas_call(
        functools.partial(spectral_kernel, blocks, rows, replicas, group, factor),
        out_shape=jax.ShapeDtypeStruct((count, group * (pair + half), LANES), jnp.bfloat16),
        in_specs=[VMEM] * 9,
        out_specs=VMEM,
        scratch_shapes=[
            pltpu.VMEM((count * group * own, LANES), jnp.float32),
            pltpu.VMEM((2 * blocks * group * half, LANES), jnp.float32),
        ],
        compiler_params=LIMIT,
        name="spectral",
    )(received, *tables)
    returned = lax.all_to_all(results, everyone, split_axis=0, concat_axis=0, tiled=True)
    own_taps = returned[:, group * pair :, :]
    other_taps = lax.ppermute(own_taps, "dp", [(i, i ^ 1) for i in range(replicas)])
    conv_out, signal_grad = pl.pallas_call(
        functools.partial(unpack_kernel, group),
        out_shape=[jax.ShapeDtypeStruct(signal.shape, jnp.bfloat16)] * 2,
        in_specs=[SMEM, VMEM],
        out_specs=[VMEM, VMEM],
        scratch_shapes=[pltpu.VMEM((count * group * pair, LANES), jnp.float32)],
        compiler_params=LIMIT,
        name="unpack",
    )(block_mask, returned)
    filter_grad = pl.pallas_call(
        functools.partial(unpack_taps_kernel, group),
        out_shape=jax.ShapeDtypeStruct(filter_raw.shape, jnp.bfloat16),
        in_specs=[VMEM, VMEM],
        out_specs=VMEM,
        scratch_shapes=[pltpu.VMEM((count * group * half, LANES), jnp.float32)],
        compiler_params=LIMIT,
        name="unpack_taps",
    )(own_taps, other_taps)
    return conv_out, signal_grad, filter_grad


def solution(mesh):
    placed = (P("dp", "seq", None), P("seq", None), P("dp", "seq", None), P("dp", "seq"))
    return jax.shard_map(
        per_device,
        mesh=mesh,
        in_specs=placed,
        out_specs=(P("dp", "seq", None), P("dp", "seq", None), P("seq", None)),
        check_vma=False,
    )
```

time: 817 us -> 119 us (0.15)
  waiting for transfers between devices: 468 us -> 0.01 us
  local copies, waits for them, and re-layouts: 134 us -> 3.47 us
  matrix products: 99.5 us -> 0 us
  blocking collectives: 0 us -> 99.5 us
  starting transfers between devices: 57.1 us -> 0.07 us
  other arithmetic: 35.5 us -> 0 us
  between operations: 15.9 us -> 1.42 us
  Pallas kernels: 0 us -> 14 us
    all_to_all x12 -> x0, waiting for transfers between devices: 412 us -> none  [the longest x3 183 us: forward(): lax.all_to_all(spread, 'seq', split_axis=1, concat_axis=2, tiled=True)]
    dot_general x60 -> x0, matrix products: 99.5 us -> none  [the longest x3 11.6 us: inner_section(): jnp.einsum('pr,kpqc->krqc', sin_rad, parted[0], preferred_element_type=jn...]
    all_to_all x0 -> x2, blocking collectives: none -> 99.5 us  [the longest x1 50.1 us: per_device(): lax.all_to_all(packed, everyone, split_axis=0, concat_axis=0, tiled=True)]
    all_to_all x12 -> x0, starting transfers between devices: 56.9 us -> none  [the longest x3 17 us: forward(): lax.all_to_all(values, 'seq', split_axis=1, concat_axis=0, tiled=True)]
    psum x1 -> x0, waiting for transfers between devices: 55.4 us -> none  [per_device(): lax.psum(spec_weight.astype(jnp.bfloat16), 'dp').astype(jnp.float32)]
    unnamed x55 -> x22, local copies, waits for them, and re-layouts: 36.4 us -> 3.45 us
    slice x19 -> x1, local copies, waits for them, and re-layouts: 28.1 us -> 0.03 us  [per_device(): own_taps = returned[:, group * pair:, :]]
    another operation x6 -> x0, local copies, waits for them, and re-layouts: 21.9 us -> none  [the longest x3 14.7 us: inverse(): packed = jnp.stack([turned_real, turned_imag]).astype(jnp.bfloat16)]
  transfers between devices with their start and end apart: 13 -> 1, of which waited for: 12 -> 0; matrix products, arithmetic and copies ran while one was open for 17% -> 0% of each run, Pallas kernels for 0% -> 2%
where the time goes in v1:
time: 119 us; the launch traced here: 118 us
  blocking collectives  99.5 us (84%)
  Pallas kernels  14 us (12%)
  local copies, waits for them, and re-layouts  3.47 us (3%)
  between operations  1.42 us (1%)
    all_to_all x1, blocking collectives, per_device(): lax.all_to_all(packed, everyone, split_axis=0, concat_axis=0, tiled=True)  50.1 us
    all_to_all x1, blocking collectives, per_device(): lax.all_to_all(results, everyone, split_axis=0, concat_axis=0, tiled=True)  49.3 us
    pallas_call x1, Pallas kernels, per_device(): pl.pallas_call(functools.partial(spectral_kernel, blocks, rows, replicas,...  8.76 us
    unnamed x22, local copies, waits for them, and re-layouts  3.45 us
    pallas_call x1, Pallas kernels, per_device(): pl.pallas_call(functools.partial(unpack_kernel, group), out_shape=[jax.Sh...  2.49 us
  transfers between devices with their start and end apart: 1, of which 0 were waited for; matrix products, arithmetic and copies ran while one was open for 0% of the time, Pallas kernels for 2%

profile of v1, /device:TPU:0, one launch (start us, length us, event | category | flops | bytes accessed | tf_op | source)
XLA Modules:
  0.0 118.5 jit_solution(1852010506362930659)
XLA Ops:
  1.3 0.0 copy-start
  1.3 1.1 copy-done
  2.4 1.1 copy-done.1
  3.5 1.1 copy-done.2
  4.7 1.6 %pack.1 = bf16[32,216,128]{2,1,0:T(8,128)(2,1)S(1)} custom-call(s32[1,1]{1,0:T(1,128)S(6)} %copy.15.mask_ref, bf16[1,1024,384]{2,1,0:T(8,128)(2,1)S(1)} %copy-done, bf16[1,1024,384]{2,1,0:T(8,128)(2,1)S(1)} %copy-done.1, bf16[1024,384]{1,0:T(8,128)(2,1)S(1)} %copy-done.2), custom_call_target="tpu_custom_call" | custom-call | tf_op jit(solution)/shard_map/pack/pallas_call | solution.py:271
  6.3 0.0 copy-start.3
  6.3 0.0 copy-start.4
  6.3 0.0 copy-start.5
  6.3 0.0 copy-start.6
  6.3 0.0 copy-start.7
  6.3 0.0 copy-start.8
  6.3 0.0 copy-start.9
  6.3 0.0 copy-start.10
  6.4 50.1 %all_to_all.10.recv_ref = bf16[32,216,128]{2,1,0:T(8,128)(2,1)S(1)} all-to-all(bf16[32,216,128]{2,1,0:T(8,128)(2,1)S(1)} %pack.1), channel_id=1, replica_groups=mesh['seq'=8,'dp'=4] {'dp','seq'}, dimensions={0} | all-to-all | bytes 3538944 | tf_op jit(solution)/shard_map/all_to_all | solution.py:283
  56.5 0.0 copy-done.3
  56.5 0.0 copy-done.4
  56.5 0.0 copy-done.5
  56.5 0.0 copy-done.6
  56.6 8.8 %spectral.1 = bf16[32,240,128]{2,1,0:T(8,128)(2,1)S(1)} custom-call(bf16[32,216,128]{2,1,0:T(8,128)(2,1)S(1)} %all_to_all.10.recv_ref, bf16[256,128]{1,0:T(8,128)(2,1)S(1)} %copy-done.6, bf16[128,64]{1,0:T(8,128)(2,1)S(1)} %copy-done.9, bf16[256,256]{1,0:T(8,128)(2,1)S(1)} %copy-done.4, bf16[256,256]{1,0:T(8,128)(2,1)S(1)} %copy-done.3, ...), custom_call_target="tpu_custom_call" | custom-call | tf_op jit(solution)/shard_map/spectral/pallas_call | solution.py:284
  65.3 49.3 %all_to_all.11.recv_ref = bf16[32,240,128]{2,1,0:T(8,128)(2,1)S(1)} all-to-all(bf16[32,240,128]{2,1,0:T(8,128)(2,1)S(1)} %spectral.1), channel_id=1, replica_groups=mesh['seq'=8,'dp'=4] {'dp','seq'}, dimensions={0} | all-to-all | bytes 3932160 | tf_op jit(solution)/shard_map/all_to_all | solution.py:296
  114.7 0.1 collective-permute-start
  114.8 2.5 %unpack.1 = (bf16[1,1024,384]{2,1,0:T(8,128)(2,1)}, bf16[1,1024,384]{2,1,0:T(8,128)(2,1)}) custom-call(s32[1,1]{1,0:T(1,128)S(6)} %copy.15.mask_ref, bf16[32,240,128]{2,1,0:T(8,128)(2,1)S(1)} %all_to_all.11.recv_ref), custom_call_target="tpu_custom_call" | custom-call | tf_op jit(solution)/shard_map/unpack/pallas_call | solution.py:299
  117.2 0.0 collective-permute-done.other_ref
  117.2 1.2 %unpack_taps.1 = bf16[1024,384]{1,0:T(8,128)(2,1)} custom-call(bf16[32,48,128]{2,1,0:T(8,128)(2,1)S(1)} %slice.4.own_ref, bf16[32,48,128]{2,1,0:T(8,128)(2,1)S(1)} %collective-permute-done.other_ref), custom_call_target="tpu_custom_call" | custom-call | tf_op jit(solution)/shard_map/unpack_taps/pallas_call | solution.py:308
  (7 shorter events, 0.0 us)
Async XLA Ops:
  1.3 1.1 copy-start
  2.4 1.1 copy-start.1
  3.5 1.1 copy-start.2
  6.3 50.2 %copy-start.3 = (bf16[256,256]{1,0:T(8,128)(2,1)S(1)}, bf16[256,256]{1,0:T(8,128)(2,1)}, u32[]{:S(2)}) copy-start(bf16[256,256]{1,0:T(8,128)(2,1)} %constant.19.clone.inner_back_ref) | copy-start | bytes 393220
  6.3 50.2 %copy-start.4 = (bf16[256,256]{1,0:T(8,128)(2,1)S(1)}, bf16[256,256]{1,0:T(8,128)(2,1)}, u32[]{:S(2)}) copy-start(bf16[256,256]{1,0:T(8,128)(2,1)} %constant.18.clone.inner_ref) | copy-start | bytes 393220
  6.3 50.2 %copy-start.5 = (bf16[128,256]{1,0:T(8,128)(2,1)S(1)}, bf16[128,256]{1,0:T(8,128)(2,1)}, u32[]{:S(2)}) copy-start(bf16[128,256]{1,0:T(8,128)(2,1)} %constant.20.clone.last_ref) | copy-start | bytes 196612
  6.3 50.2 %copy-start.6 = (bf16[256,128]{1,0:T(8,128)(2,1)S(1)}, bf16[256,128]{1,0:T(8,128)(2,1)}, u32[]{:S(2)}) copy-start(bf16[256,128]{1,0:T(8,128)(2,1)} %constant.16.clone.first_ref) | copy-start | bytes 196612
  6.3 50.2 %copy-start.7 = (f32[64,128]{1,0:T(8,128)S(1)}, f32[64,128]{1,0:T(8,128)}, u32[]{:S(2)}) copy-start(f32[64,128]{1,0:T(8,128)} %constant.23.clone.twist_sin_ref) | copy-start | bytes 98308
  6.3 50.2 %copy-start.8 = (f32[64,128]{1,0:T(8,128)S(1)}, f32[64,128]{1,0:T(8,128)}, u32[]{:S(2)}) copy-start(f32[64,128]{1,0:T(8,128)} %constant.22.clone.twist_cos_ref) | copy-start | bytes 98308
  6.3 50.2 %copy-start.9 = (bf16[128,64]{1,0:T(8,128)(2,1)S(1)}, bf16[128,64]{1,0:T(8,128)(2,1)}, u32[]{:S(2)}) copy-start(bf16[128,64]{1,0:T(8,128)(2,1)} %constant.17.clone.first_taps_ref) | copy-start | bytes 49156
  6.3 50.2 %copy-start.10 = (bf16[64,128]{1,0:T(8,128)(2,1)S(1)}, bf16[64,128]{1,0:T(8,128)(2,1)}, u32[]{:S(2)}) copy-start(bf16[64,128]{1,0:T(8,128)(2,1)} %constant.21.clone.last_taps_ref) | copy-start | bytes 49156
  114.7 2.6 %collective-permute-start = (bf16[32,48,128]{2,1,0:T(8,128)(2,1)S(1)}, bf16[32,48,128]{2,1,0:T(8,128)(2,1)S(1)}, u32[]{:S(2)}, u32[]{:S(2)}) collective-permute-start(bf16[32,48,128]{2,1,0:T(8,128)(2,1)S(1)} %slice.4.own_ref), channel_id=1, source_target_pairs={{0,1},{1,0},{2,3},{3,2},{4,5},{5,4},{6,7},{7,6},{8,9},{9,8},{10,11... | collective-permute-start | bytes 1179656 | tf_op jit(solution)/shard_map/ppermute | solution.py:298

commit v2 on v1

--- a/solution.py
+++ b/solution.py
@@ -38,8 +38,8 @@
         last[:, which, :, which, 1, :] = -np.moveaxis(sin_a[:, plain], 0, 2)
     taps = (
         np.arange(own)[:, None, None]
-        + own * np.arange(replicas)[None, :, None]
-        + rows * np.arange(blocks)[None, None, :]
+        + rows * np.arange(blocks)[None, :, None]
+        + own * np.arange(replicas)[None, None, :]
     ).reshape(-1)
     first_taps = np.concatenate([cos_a[:, taps], -sin_a[:, taps]], axis=0)
     back = (
@@ -66,34 +66,76 @@
     )
 
 
-def pack_kernel(own, group, count, mask_ref, signal_ref, grad_ref, filter_ref, send_ref, pair_scr, tap_scr):
+def pack_kernel(
+    own, group, count, mask_ref, signal_ref, grad_ref, filter_ref, send_ref,
+    signal_buf, grad_buf, filter_buf, send_buf, pair_scr, tap_scr, in_sems, out_sems,
+):
     tokens, channels = filter_ref.shape
     rows = tokens // LANES
     pair = 2 * rows
     block_rows = BLK // LANES
+    parts = in_sems.shape[0] // 2
+    part_rows = rows // parts
+    start = pl.multiple_of(lax.axis_index("dp") * (own * LANES), own * LANES)
+    filter_copy = pltpu.make_async_copy(
+        filter_ref.at[pl.ds(start, own * LANES), :], filter_buf, in_sems.at[2 * parts]
+    )
+    copies = []
+    for part in range(parts):
+        span = pl.ds(part * part_rows * LANES, part_rows * LANES)
+        copies.append(
+            pltpu.make_async_copy(
+                signal_ref.at[0, span, :], signal_buf.at[span, :], in_sems.at[2 * part]
+            )
+        )
+        copies.append(
+            pltpu.make_async_copy(
+                grad_ref.at[0, span, :], grad_buf.at[span, :], in_sems.at[2 * part + 1]
+            )
+        )
+    filter_copy.start()
+    for copy in copies:
+        copy.start()
     if group * count != channels:
         pair_scr[...] = jnp.zeros_like(pair_scr)
         tap_scr[...] = jnp.zeros_like(tap_scr)
-    for row in range(rows):
-        span = pl.ds(row * LANES, LANES)
-        keep = mask_ref[0, row // block_rows].astype(jnp.float32)
-        pair_scr[pl.ds(row, channels, stride=pair), :] = (
-            signal_ref[0, span, :].astype(jnp.float32).T * keep
-        )
-        pair_scr[pl.ds(rows + row, channels, stride=pair), :] = (
-            grad_ref[0, span, :].astype(jnp.float32).T
-        )
-    start = lax.axis_index("dp") * (own * LANES)
+    filter_copy.wait()
     for row in range(own):
-        span = pl.ds(pl.multiple_of(start + row * LANES, LANES), LANES)
-        tap_scr[pl.ds(row, channels, stride=own), :] = filter_ref[span, :].astype(jnp.float32).T
+        tap_scr[pl.ds(row, channels, stride=own), :] = (
+            filter_buf[row * LANES : (row + 1) * LANES, :].astype(jnp.float32).T
+        )
+    for part in range(parts):
+        places = range(part * part_rows, (part + 1) * part_rows)
+        copies[2 * part].wait()
+        for row in places:
+            keep = mask_ref[0, row // block_rows].astype(jnp.float32)
+            pair_scr[pl.ds(row, channels, stride=pair), :] = (
+                signal_buf[row * LANES : (row + 1) * LANES, :].astype(jnp.float32).T * keep
+            )
+        copies[2 * part + 1].wait()
+        for row in places:
+            pair_scr[pl.ds(rows + row, channels, stride=pair), :] = (
+                grad_buf[row * LANES : (row + 1) * LANES, :].astype(jnp.float32).T
+            )
+    batch = count // out_sems.shape[0]
+    sends = []
     for target in range(count):
-        send_ref[target, : group * pair, :] = pair_scr[
+        send_buf[target, : group * pair, :] = pair_scr[
             target * group * pair : (target + 1) * group * pair, :
         ].astype(jnp.bfloat16)
-        send_ref[target, group * pair :, :] = tap_scr[
+        send_buf[target, group * pair :, :] = tap_scr[
             target * group * own : (target + 1) * group * own, :
         ].astype(jnp.bfloat16)
+        if target % batch == batch - 1:
+            span = pl.ds(target + 1 - batch, batch)
+            sends.append(
+                pltpu.make_async_copy(
+                    send_buf.at[span], send_ref.at[span], out_sems.at[target // batch]
+                )
+            )
+            sends[-1].start()
+    for copy in sends:
+        copy.wait()
 
 
 def spectral_kernel(
@@ -133,8 +175,12 @@
         spread_taps = dot(first_taps_ref[...], taps)
         data = jnp.concatenate(
             [
-                recv_ref[seq * blocks : (seq + 1) * blocks, pl.ds(offset, pair), :].reshape(
-                    blocks * pair, LANES
+                jnp.concatenate(
+                    [
+                        recv_ref[block * replicas + seq, pl.ds(offset, pair), :]
+                        for block in range(blocks)
+                    ],
+                    axis=0,
                 )
                 for seq in range(replicas)
             ],
@@ -196,9 +242,10 @@
         )
         result = (dot(last_ref[...], columns) * factor).astype(jnp.bfloat16)
         for seq in range(replicas):
-            send_ref[seq * blocks : (seq + 1) * blocks, pl.ds(offset, pair), :] = result[
-                :, seq * LANES : (seq + 1) * LANES
-            ].reshape(blocks, pair, LANES)
+            for block in range(blocks):
+                send_ref[block * replicas + seq, pl.ds(offset, pair), :] = result[
+                    block * pair : (block + 1) * pair, seq * LANES : (seq + 1) * LANES
+                ]
         weights = dot(last_taps_ref[...], turn_back(2 * replicas)) * factor
         for row in range(half):
             back_scr[pl.ds(index * half + row, 2 * blocks, stride=back_rows), :] = weights[
@@ -206,15 +253,17 @@
             ]
         return carry
 
-    lax.fori_loop(0, group, channel, 0)
+    lax.fori_loop(0, group, channel, 0, unroll=min(group, 12))
     for target in range(count):
-        place = (target // blocks) % 2 * blocks + target % blocks
+        place = target % replicas % 2 * blocks + target // replicas
         send_ref[target, group * pair :, :] = back_scr[
             place * back_rows : (place + 1) * back_rows, :
         ].astype(jnp.bfloat16)
 
 
-def unpack_kernel(group, mask_ref, recv_ref, conv_ref, grad_ref, pair_scr):
+def unpack_kernel(
+    group, mask_ref, recv_ref, conv_ref, grad_ref, pair_scr, conv_buf, grad_buf, sems
+):
     tokens, channels = conv_ref.shape[1:]
     rows = tokens // LANES
     pair = 2 * rows
@@ -224,31 +273,59 @@
         pair_scr[source * size : (source + 1) * size, :] = recv_ref[source, :size, :].astype(
             jnp.float32
         )
+    copies = []
     for row in range(rows):
         span = pl.ds(row * LANES, LANES)
         keep = mask_ref[0, row // block_rows].astype(jnp.float32)
-        conv_ref[0, span, :] = pair_scr[pl.ds(row, channels, stride=pair), :].T.astype(jnp.bfloat16)
-        grad_ref[0, span, :] = (
+        conv_buf[span, :] = pair_scr[pl.ds(row, channels, stride=pair), :].T.astype(jnp.bfloat16)
+        copies.append(
+            pltpu.make_async_copy(conv_buf.at[span, :], conv_ref.at[0, span, :], sems.at[2 * row])
+        )
+        copies[-1].start()
+        grad_buf[span, :] = (
             pair_scr[pl.ds(rows + row, channels, stride=pair), :].T * keep
         ).astype(jnp.bfloat16)
-
-
-def unpack_taps_kernel(group, own_ref, other_ref, taps_ref, scr):
+        copies.append(
+            pltpu.make_async_copy(
+                grad_buf.at[span, :], grad_ref.at[0, span, :], sems.at[2 * row + 1]
+            )
+        )
+        copies[-1].start()
+    for copy in copies:
+        copy.wait()
+
+
+def unpack_taps_kernel(group, own_ref, other_ref, taps_ref, scr, taps_buf, sems):
     tokens, channels = taps_ref.shape
     half = tokens // LANES // 2
     size = group * half
     side = lax.rem(lax.axis_index("dp"), 2)
+    copies = []
     for place, ref in enumerate((own_ref, other_ref)):
+        base = place * ref.shape[0] * size
         for source in range(ref.shape[0]):
-            scr[source * size : (source + 1) * size, :] = ref[source].astype(jnp.float32)
+            scr[base + source * size : base + (source + 1) * size, :] = ref[source].astype(
+                jnp.float32
+            )
         start = jnp.where(side == place, 0, half * LANES)
         for row in range(half):
-            span = pl.ds(pl.multiple_of(start + row * LANES, LANES), LANES)
-            taps_ref[span, :] = scr[pl.ds(row, channels, stride=half), :].T.astype(jnp.bfloat16)
+            slot = place * half + row
+            span = pl.ds(slot * LANES, LANES)
+            taps_buf[span, :] = scr[pl.ds(base + row, channels, stride=half), :].T.astype(
+                jnp.bfloat16
+            )
+            goal = pl.ds(pl.multiple_of(start + row * LANES, LANES), LANES)
+            copies.append(
+                pltpu.make_async_copy(taps_buf.at[span, :], taps_ref.at[goal, :], sems.at[slot])
+            )
+            copies[-1].start()
+    for copy in copies:
+        copy.wait()
 
 
 VMEM = pl.BlockSpec(memory_space=pltpu.VMEM)
 SMEM = pl.BlockSpec(memory_space=pltpu.SMEM)
+HBM = pl.BlockSpec(memory_space=pltpu.HBM)
 LIMIT = pltpu.CompilerParams(vmem_limit_bytes=48 * 1024 * 1024)
 
 
@@ -265,19 +342,25 @@
     total = tokens * blocks
     coarse = total // LANES
     factor = 1.0 / (total * math.sqrt(total))
-    everyone = ("dp", "seq")
+    everyone = ("seq", "dp")
     tables = [jnp.asarray(t) for t in make_tables(blocks, rows, replicas)]
 
     packed = pl.pallas_call(
         functools.partial(pack_kernel, own, group, count),
         out_shape=jax.ShapeDtypeStruct((count, group * (pair + own), LANES), jnp.bfloat16),
-        in_specs=[SMEM, VMEM, VMEM, VMEM],
-        out_specs=VMEM,
+        in_specs=[SMEM, HBM, HBM, HBM],
+        out_specs=HBM,
         scratch_shapes=[
+            pltpu.VMEM((tokens, channels), jnp.bfloat16),
+            pltpu.VMEM((tokens, channels), jnp.bfloat16),
+            pltpu.VMEM((own * LANES, channels), jnp.bfloat16),
+            pltpu.VMEM((count, group * (pair + own), LANES), jnp.bfloat16),
             pltpu.VMEM((count * group * pair, LANES), jnp.float32),
             pltpu.VMEM((count * group * own, LANES), jnp.float32),
+            pltpu.SemaphoreType.DMA((5,)),
+            pltpu.SemaphoreType.DMA((4,)),
         ],
-        compiler_params=LIMIT,
+        compiler_params=pltpu.CompilerParams(vmem_limit_bytes=60 * 1024 * 1024),
         name="pack",
     )(block_mask, signal, cotangent, filter_raw)
     received = lax.all_to_all(packed, everyone, split_axis=0, concat_axis=0, tiled=True)
@@ -300,8 +383,13 @@
         functools.partial(unpack_kernel, group),
         out_shape=[jax.ShapeDtypeStruct(signal.shape, jnp.bfloat16)] * 2,
         in_specs=[SMEM, VMEM],
-        out_specs=[VMEM, VMEM],
-        scratch_shapes=[pltpu.VMEM((count * group * pair, LANES), jnp.float32)],
+        out_specs=[HBM, HBM],
+        scratch_shapes=[
+            pltpu.VMEM((count * group * pair, LANES), jnp.float32),
+            pltpu.VMEM((tokens, channels), jnp.bfloat16),
+            pltpu.VMEM((tokens, channels), jnp.bfloat16),
+            pltpu.SemaphoreType.DMA((2 * rows,)),
+        ],
         compiler_params=LIMIT,
         name="unpack",
     )(block_mask, returned)
@@ -309,8 +397,12 @@
         functools.partial(unpack_taps_kernel, group),
         out_shape=jax.ShapeDtypeStruct(filter_raw.shape, jnp.bfloat16),
         in_specs=[VMEM, VMEM],
-        out_specs=VMEM,
-        scratch_shapes=[pltpu.VMEM((count * group * half, LANES), jnp.float32)],
+        out_specs=HBM,
+        scratch_shapes=[
+            pltpu.VMEM((2 * count * group * half, LANES), jnp.float32),
+            pltpu.VMEM((tokens, channels), jnp.bfloat16),
+            pltpu.SemaphoreType.DMA((2 * half,)),
+        ],
         compiler_params=LIMIT,
         name="unpack_taps",
     )(own_taps, other_taps)

time: 119 us -> 115 us (0.966)
  local copies, waits for them, and re-layouts: 3.47 us -> 0.08 us
  blocking collectives: 99.5 us -> 98.3 us
    unnamed x22 -> x16, local copies, waits for them, and re-layouts: 3.45 us -> 0.05 us
    pallas_call x1, Pallas kernels: 1.57 us -> 4.06 us  [per_device(): pl.pallas_call(functools.partial(pack_kernel, own, group, count), out_sha...]
    pallas_call x1, Pallas kernels: 8.76 us -> 7.27 us  [per_device(): pl.pallas_call(functools.partial(spectral_kernel, blocks, rows, replicas,...]
where the time goes in v2:
time: 115 us
  blocking collectives  98.3 us (85%)
  Pallas kernels  14.6 us (13%)
  between operations  1.43 us (1%)
    all_to_all x1, blocking collectives, per_device(): lax.all_to_all(results, everyone, split_axis=0, concat_axis=0, tiled=True)  49.3 us
    all_to_all x1, blocking collectives, per_device(): lax.all_to_all(packed, everyone, split_axis=0, concat_axis=0, tiled=True)  49 us
    pallas_call x1, Pallas kernels, per_device(): pl.pallas_call(functools.partial(spectral_kernel, blocks, rows, replicas,...  7.27 us
    pallas_call x1, Pallas kernels, per_device(): pl.pallas_call(functools.partial(pack_kernel, own, group, count), out_sha...  4.06 us
  transfers between devices with their start and end apart: 1, of which 0 were waited for; matrix products, arithmetic and copies ran while one was open for 0% of the time, Pallas kernels for 2%

profile of v2, /device:TPU:0, one launch (start us, length us, event | category | flops | bytes accessed | tf_op | source)
XLA Modules:
  0.0 114.5 jit_solution(7435260079741670383)
XLA Ops:
  1.3 4.1 %pack.1 = bf16[32,216,128]{2,1,0:T(8,128)(2,1)} custom-call(s32[1,1]{1,0:T(1,128)S(6)} %copy.15.mask_ref, bf16[1,1024,384]{2,1,0:T(8,128)(2,1)} %signal_ref.1, bf16[1,1024,384]{2,1,0:T(8,128)(2,1)} %grad_ref.1, bf16[1024,384]{1,0:T(8,128)(2,1)} %filter_ref.1), custom_call_target="tpu_custom_call" | custom-call | tf_op jit(solution)/shard_map/pack/pallas_call | solution.py:348
  5.3 0.0 copy-start
  5.4 0.0 copy-start.1
  5.4 0.0 copy-start.2
  5.4 0.0 copy-start.3
  5.4 0.0 copy-start.4
  5.4 0.0 copy-start.5
  5.4 0.0 copy-start.6
  5.4 0.0 copy-start.7
  5.4 49.0 %all_to_all.10.recv_ref = bf16[32,216,128]{2,1,0:T(8,128)(2,1)S(1)} all-to-all(bf16[32,216,128]{2,1,0:T(8,128)(2,1)} %pack.1), channel_id=1, replica_groups=mesh['seq'=8,'dp'=4] {'seq','dp'}, dimensions={0} | all-to-all | bytes 3538944 | tf_op jit(solution)/shard_map/all_to_all | solution.py:366
  54.4 0.0 copy-done
  54.4 0.0 copy-done.1
  54.5 0.0 copy-done.2
  54.5 0.0 copy-done.3
  54.5 0.0 copy-done.4
  54.5 0.0 copy-done.5
  54.5 0.0 copy-done.6
  54.5 0.0 copy-done.7
  54.5 7.3 %spectral.1 = bf16[32,240,128]{2,1,0:T(8,128)(2,1)S(1)} custom-call(bf16[32,216,128]{2,1,0:T(8,128)(2,1)S(1)} %all_to_all.10.recv_ref, bf16[256,128]{1,0:T(8,128)(2,1)S(1)} %copy-done.3, bf16[128,64]{1,0:T(8,128)(2,1)S(1)} %copy-done.6, bf16[256,256]{1,0:T(8,128)(2,1)S(1)} %copy-done.1, bf16[256,256]{1,0:T(8,128)(2,1)S(1)} %copy-done, ...), custom_call_target="tpu_custom_call" | custom-call | tf_op jit(solution)/shard_map/spectral/pallas_call | solution.py:367
  61.8 49.3 %all_to_all.11.recv_ref = bf16[32,240,128]{2,1,0:T(8,128)(2,1)S(1)} all-to-all(bf16[32,240,128]{2,1,0:T(8,128)(2,1)S(1)} %spectral.1), channel_id=1, replica_groups=mesh['seq'=8,'dp'=4] {'seq','dp'}, dimensions={0} | all-to-all | bytes 3932160 | tf_op jit(solution)/shard_map/all_to_all | solution.py:379
  111.1 0.1 collective-permute-start
  111.2 2.2 %unpack.1 = (bf16[1,1024,384]{2,1,0:T(8,128)(2,1)}, bf16[1,1024,384]{2,1,0:T(8,128)(2,1)}) custom-call(s32[1,1]{1,0:T(1,128)S(6)} %copy.15.mask_ref, bf16[32,240,128]{2,1,0:T(8,128)(2,1)S(1)} %all_to_all.11.recv_ref), custom_call_target="tpu_custom_call" | custom-call | tf_op jit(solution)/shard_map/unpack/pallas_call | solution.py:382
  113.4 0.0 collective-permute-done.other_ref
  113.4 1.1 unpack_taps.1
  (1 shorter events, 0.0 us)
Async XLA Ops:
  5.3 49.1 %copy-start = (bf16[256,256]{1,0:T(8,128)(2,1)S(1)}, bf16[256,256]{1,0:T(8,128)(2,1)}, u32[]{:S(2)}) copy-start(bf16[256,256]{1,0:T(8,128)(2,1)} %constant.19.clone.inner_back_ref) | copy-start | bytes 393220
  5.4 49.1 %copy-start.1 = (bf16[256,256]{1,0:T(8,128)(2,1)S(1)}, bf16[256,256]{1,0:T(8,128)(2,1)}, u32[]{:S(2)}) copy-start(bf16[256,256]{1,0:T(8,128)(2,1)} %constant.18.clone.inner_ref) | copy-start | bytes 393220
  5.4 49.1 %copy-start.2 = (bf16[128,256]{1,0:T(8,128)(2,1)S(1)}, bf16[128,256]{1,0:T(8,128)(2,1)}, u32[]{:S(2)}) copy-start(bf16[128,256]{1,0:T(8,128)(2,1)} %constant.20.clone.last_ref) | copy-start | bytes 196612
  5.4 49.1 %copy-start.3 = (bf16[256,128]{1,0:T(8,128)(2,1)S(1)}, bf16[256,128]{1,0:T(8,128)(2,1)}, u32[]{:S(2)}) copy-start(bf16[256,128]{1,0:T(8,128)(2,1)} %constant.16.clone.first_ref) | copy-start | bytes 196612
  5.4 49.1 %copy-start.4 = (f32[64,128]{1,0:T(8,128)S(1)}, f32[64,128]{1,0:T(8,128)}, u32[]{:S(2)}) copy-start(f32[64,128]{1,0:T(8,128)} %constant.23.clone.twist_sin_ref) | copy-start | bytes 98308
  5.4 49.1 %copy-start.5 = (f32[64,128]{1,0:T(8,128)S(1)}, f32[64,128]{1,0:T(8,128)}, u32[]{:S(2)}) copy-start(f32[64,128]{1,0:T(8,128)} %constant.22.clone.twist_cos_ref) | copy-start | bytes 98308
  5.4 49.1 %copy-start.6 = (bf16[128,64]{1,0:T(8,128)(2,1)S(1)}, bf16[128,64]{1,0:T(8,128)(2,1)}, u32[]{:S(2)}) copy-start(bf16[128,64]{1,0:T(8,128)(2,1)} %constant.17.clone.first_taps_ref) | copy-start | bytes 49156
  5.4 49.1 %copy-start.7 = (bf16[64,128]{1,0:T(8,128)(2,1)S(1)}, bf16[64,128]{1,0:T(8,128)(2,1)}, u32[]{:S(2)}) copy-start(bf16[64,128]{1,0:T(8,128)(2,1)} %constant.21.clone.last_taps_ref) | copy-start | bytes 49156
  111.1 2.3 %collective-permute-start = (bf16[32,48,128]{2,1,0:T(8,128)(2,1)S(1)}, bf16[32,48,128]{2,1,0:T(8,128)(2,1)S(1)}, u32[]{:S(2)}, u32[]{:S(2)}) collective-permute-start(bf16[32,48,128]{2,1,0:T(8,128)(2,1)S(1)} %slice.4.own_ref), channel_id=1, source_target_pairs={{0,1},{1,0},{2,3},{3,2},{4,5},{5,4},{6,7},{7,6},{8,9},{9,8},{10,11... | collective-permute-start | bytes 1179656 | tf_op jit(solution)/shard_map/ppermute | solution.py:381

commit v3 on v2

--- a/solution.py
+++ b/solution.py
@@ -68,7 +68,7 @@
 
 def pack_kernel(
     own, group, count, mask_ref, signal_ref, grad_ref, filter_ref, send_ref,
-    signal_buf, grad_buf, filter_buf, send_buf, pair_scr, tap_scr, in_sems, out_sems,
+    signal_buf, grad_buf, filter_buf, pair_scr, tap_scr, in_sems,
 ):
     tokens, channels = filter_ref.shape
     rows = tokens // LANES
@@ -117,25 +117,13 @@
             pair_scr[pl.ds(rows + row, channels, stride=pair), :] = (
                 grad_buf[row * LANES : (row + 1) * LANES, :].astype(jnp.float32).T
             )
-    batch = count // out_sems.shape[0]
-    sends = []
     for target in range(count):
-        send_buf[target, : group * pair, :] = pair_scr[
+        send_ref[target, : group * pair, :] = pair_scr[
             target * group * pair : (target + 1) * group * pair, :
         ].astype(jnp.bfloat16)
-        send_buf[target, group * pair :, :] = tap_scr[
+        send_ref[target, group * pair :, :] = tap_scr[
             target * group * own : (target + 1) * group * own, :
         ].astype(jnp.bfloat16)
-        if target % batch == batch - 1:
-            span = pl.ds(target + 1 - batch, batch)
-            sends.append(
-                pltpu.make_async_copy(
-                    send_buf.at[span], send_ref.at[span], out_sems.at[target // batch]
-                )
-            )
-            sends[-1].start()
-    for copy in sends:
-        copy.wait()
 
 
 def spectral_kernel(
@@ -158,8 +146,8 @@
     def dot(left, right):
         return jnp.dot(left, right, preferred_element_type=jnp.float32)
 
-    def channel(index, carry):
-        offset = pl.multiple_of(index * pair, pair)
+    def spread(index):
+        offset = index * pair
         twist_cos = twist_cos_ref[...]
         twist_sin = twist_sin_ref[...]
 
@@ -172,7 +160,7 @@
             [tap_scr[pl.ds(index * own + row, count, stride=tap_rows), :] for row in range(own)],
             axis=0,
         ).astype(jnp.bfloat16)
-        spread_taps = dot(first_taps_ref[...], taps)
+        wide_taps = dot(first_taps_ref[...], taps)
         data = jnp.concatenate(
             [
                 jnp.concatenate(
@@ -186,16 +174,19 @@
             ],
             axis=1,
         )
-        spread = dot(first_ref[...], data)
-        turned = [turn(spread_taps[:coarse], spread_taps[coarse:])]
+        wide = dot(first_ref[...], data)
+        turned = [turn(wide_taps[:coarse], wide_taps[coarse:])]
         for seq in range(replicas):
-            part = spread[:, seq * LANES : (seq + 1) * LANES]
+            part = wide[:, seq * LANES : (seq + 1) * LANES]
             for which in range(2):
                 base = 2 * which * coarse
                 turned.append(
                     turn(part[base : base + coarse], part[base + coarse : base + 2 * coarse])
                 )
-        spectrum = dot(jnp.concatenate(turned, axis=0), inner_ref[...])
+        return jnp.concatenate(turned, axis=0)
+
+    def multiply(turned):
+        spectrum = dot(turned, inner_ref[...])
 
         def pick(place):
             piece = spectrum[place * coarse : (place + 1) * coarse]
@@ -224,7 +215,12 @@
         products.append(
             jnp.concatenate([weight_real, weight_imag], axis=1).astype(jnp.bfloat16)
         )
-        inverted = dot(jnp.concatenate(products, axis=0), inner_back_ref[...])
+        return jnp.concatenate(products, axis=0)
+
+    def narrow(products):
+        inverted = dot(products, inner_back_ref[...])
+        twist_cos = twist_cos_ref[...]
+        twist_sin = twist_sin_ref[...]
 
         def turn_back(place):
             piece = inverted[place * coarse : (place + 1) * coarse]
@@ -240,20 +236,32 @@
             ],
             axis=1,
         )
+        return columns, turn_back(2 * replicas)
+
+    def finish(index, columns, weight_column):
+        offset = index * pair
         result = (dot(last_ref[...], columns) * factor).astype(jnp.bfloat16)
         for seq in range(replicas):
             for block in range(blocks):
                 send_ref[block * replicas + seq, pl.ds(offset, pair), :] = result[
                     block * pair : (block + 1) * pair, seq * LANES : (seq + 1) * LANES
                 ]
-        weights = dot(last_taps_ref[...], turn_back(2 * replicas)) * factor
+        weights = dot(last_taps_ref[...], weight_column) * factor
         for row in range(half):
             back_scr[pl.ds(index * half + row, 2 * blocks, stride=back_rows), :] = weights[
                 row * 2 * blocks : (row + 1) * 2 * blocks
             ]
-        return carry
-
-    lax.fori_loop(0, group, channel, 0, unroll=min(group, 12))
+
+    turned, products, columns = {}, {}, {}
+    for step in range(group + 3):
+        if step >= 3:
+            finish(step - 3, *columns.pop(step - 3))
+        if 2 <= step < group + 2:
+            columns[step - 2] = narrow(products.pop(step - 2))
+        if 1 <= step < group + 1:
+            products[step - 1] = multiply(turned.pop(step - 1))
+        if step < group:
+            turned[step] = spread(step)
     for target in range(count):
         place = target % replicas % 2 * blocks + target // replicas
         send_ref[target, group * pair :, :] = back_scr[
@@ -345,24 +353,23 @@
     everyone = ("seq", "dp")
     tables = [jnp.asarray(t) for t in make_tables(blocks, rows, replicas)]
 
+    inputs = (signal, cotangent, filter_raw)
     packed = pl.pallas_call(
         functools.partial(pack_kernel, own, group, count),
-        out_shape=jax.ShapeDtypeStruct((count, group * (pair + own), LANES), jnp.bfloat16),
+        out_shape=pltpu.VMEM((count, group * (pair + own), LANES), jnp.bfloat16),
         in_specs=[SMEM, HBM, HBM, HBM],
-        out_specs=HBM,
+        out_specs=VMEM,
         scratch_shapes=[
             pltpu.VMEM((tokens, channels), jnp.bfloat16),
             pltpu.VMEM((tokens, channels), jnp.bfloat16),
             pltpu.VMEM((own * LANES, channels), jnp.bfloat16),
-            pltpu.VMEM((count, group * (pair + own), LANES), jnp.bfloat16),
             pltpu.VMEM((count * group * pair, LANES), jnp.float32),
             pltpu.VMEM((count * group * own, LANES), jnp.float32),
             pltpu.SemaphoreType.DMA((5,)),
-            pltpu.SemaphoreType.DMA((4,)),
         ],
-        compiler_params=pltpu.CompilerParams(vmem_limit_bytes=60 * 1024 * 1024),
+        compiler_params=LIMIT,
         name="pack",
-    )(block_mask, signal, cotangent, filter_raw)
+    )(block_mask, *(pltpu.with_memory_space_constraint(x, pltpu.HBM) for x in inputs))
     received = lax.all_to_all(packed, everyone, split_axis=0, concat_axis=0, tiled=True)
     results = pl.pallas_call(
         functools.partial(spectral_kernel, blocks, rows, replicas, group, factor),

time: 115 us -> 111 us (0.965)
  Pallas kernels: 14.6 us -> 10.7 us
    pallas_call x1, Pallas kernels: 7.27 us -> 4.55 us  [per_device(): pl.pallas_call(functools.partial(spectral_kernel, blocks, rows, replicas,...]
    pallas_call x1, Pallas kernels: 4.06 us -> 2.82 us  [per_device(): pl.pallas_call(functools.partial(pack_kernel, own, group, count), out_sha...]
where the time goes in v3:
time: 111 us; the launch traced here: 110 us
  blocking collectives  98.1 us (88%)
  Pallas kernels  10.7 us (10%)
  between operations  1.43 us (1%)
    all_to_all x1, blocking collectives, per_device(): lax.all_to_all(results, everyone, split_axis=0, concat_axis=0, tiled=True)  49.3 us
    all_to_all x1, blocking collectives, per_device(): lax.all_to_all(packed, everyone, split_axis=0, concat_axis=0, tiled=True)  48.8 us
    pallas_call x1, Pallas kernels, per_device(): pl.pallas_call(functools.partial(spectral_kernel, blocks, rows, replicas,...  4.55 us
    pallas_call x1, Pallas kernels, per_device(): pl.pallas_call(functools.partial(pack_kernel, own, group, count), out_sha...  2.82 us
  transfers between devices with their start and end apart: 1, of which 0 were waited for; matrix products, arithmetic and copies ran while one was open for 0% of the time, Pallas kernels for 2%

profile of v3, /device:TPU:0, one launch (start us, length us, event | category | flops | bytes accessed | tf_op | source)
XLA Modules:
  0.0 110.4 jit_solution(4614381341974374219)
XLA Ops:
  1.3 2.8 %pack.1 = bf16[32,216,128]{2,1,0:T(8,128)(2,1)S(1)} custom-call(s32[1,1]{1,0:T(1,128)S(6)} %copy.15.mask_ref, bf16[1,1024,384]{2,1,0:T(8,128)(2,1)} %signal_ref.1, bf16[1,1024,384]{2,1,0:T(8,128)(2,1)} %grad_ref.1, bf16[1024,384]{1,0:T(8,128)(2,1)} %filter_ref.1), custom_call_target="tpu_custom_call" | custom-call | tf_op jit(solution)/shard_map/pack/pallas_call | solution.py:357
  4.1 0.0 copy-start
  4.1 0.0 copy-start.1
  4.1 0.0 copy-start.2
  4.1 0.0 copy-start.3
  4.2 0.0 copy-start.4
  4.2 0.0 copy-start.5
  4.2 0.0 copy-start.6
  4.2 0.0 copy-start.7
  4.2 48.8 %all_to_all.10.recv_ref = bf16[32,216,128]{2,1,0:T(8,128)(2,1)S(1)} all-to-all(bf16[32,216,128]{2,1,0:T(8,128)(2,1)S(1)} %pack.1), channel_id=1, replica_groups=mesh['seq'=8,'dp'=4] {'seq','dp'}, dimensions={0} | all-to-all | bytes 3538944 | tf_op jit(solution)/shard_map/all_to_all | solution.py:373
  53.0 0.0 copy-done
  53.0 0.0 copy-done.1
  53.0 0.0 copy-done.2
  53.0 0.0 copy-done.3
  53.0 0.0 copy-done.4
  53.0 0.0 copy-done.5
  53.0 0.0 copy-done.6
  53.0 0.0 copy-done.7
  53.1 4.6 %spectral.1 = bf16[32,240,128]{2,1,0:T(8,128)(2,1)S(1)} custom-call(bf16[32,216,128]{2,1,0:T(8,128)(2,1)S(1)} %all_to_all.10.recv_ref, bf16[256,128]{1,0:T(8,128)(2,1)S(1)} %copy-done.3, bf16[128,64]{1,0:T(8,128)(2,1)S(1)} %copy-done.6, bf16[256,256]{1,0:T(8,128)(2,1)S(1)} %copy-done.1, bf16[256,256]{1,0:T(8,128)(2,1)S(1)} %copy-done, ...), custom_call_target="tpu_custom_call" | custom-call | tf_op jit(solution)/shard_map/spectral/pallas_call | solution.py:374
  57.6 49.3 %all_to_all.11.recv_ref = bf16[32,240,128]{2,1,0:T(8,128)(2,1)S(1)} all-to-all(bf16[32,240,128]{2,1,0:T(8,128)(2,1)S(1)} %spectral.1), channel_id=1, replica_groups=mesh['seq'=8,'dp'=4] {'seq','dp'}, dimensions={0} | all-to-all | bytes 3932160 | tf_op jit(solution)/shard_map/all_to_all | solution.py:386
  107.0 0.1 collective-permute-start
  107.1 2.2 %unpack.1 = (bf16[1,1024,384]{2,1,0:T(8,128)(2,1)}, bf16[1,1024,384]{2,1,0:T(8,128)(2,1)}) custom-call(s32[1,1]{1,0:T(1,128)S(6)} %copy.15.mask_ref, bf16[32,240,128]{2,1,0:T(8,128)(2,1)S(1)} %all_to_all.11.recv_ref), custom_call_target="tpu_custom_call" | custom-call | tf_op jit(solution)/shard_map/unpack/pallas_call | solution.py:389
  109.3 0.0 collective-permute-done.other_ref
  109.3 1.1 unpack_taps.1
  (1 shorter events, 0.0 us)
Async XLA Ops:
  4.1 48.9 %copy-start = (bf16[256,256]{1,0:T(8,128)(2,1)S(1)}, bf16[256,256]{1,0:T(8,128)(2,1)}, u32[]{:S(2)}) copy-start(bf16[256,256]{1,0:T(8,128)(2,1)} %constant.19.clone.inner_back_ref) | copy-start | bytes 393220
  4.1 48.9 %copy-start.1 = (bf16[256,256]{1,0:T(8,128)(2,1)S(1)}, bf16[256,256]{1,0:T(8,128)(2,1)}, u32[]{:S(2)}) copy-start(bf16[256,256]{1,0:T(8,128)(2,1)} %constant.18.clone.inner_ref) | copy-start | bytes 393220
  4.1 48.9 %copy-start.2 = (bf16[128,256]{1,0:T(8,128)(2,1)S(1)}, bf16[128,256]{1,0:T(8,128)(2,1)}, u32[]{:S(2)}) copy-start(bf16[128,256]{1,0:T(8,128)(2,1)} %constant.20.clone.last_ref) | copy-start | bytes 196612
  4.1 48.9 %copy-start.3 = (bf16[256,128]{1,0:T(8,128)(2,1)S(1)}, bf16[256,128]{1,0:T(8,128)(2,1)}, u32[]{:S(2)}) copy-start(bf16[256,128]{1,0:T(8,128)(2,1)} %constant.16.clone.first_ref) | copy-start | bytes 196612
  4.2 48.9 %copy-start.4 = (f32[64,128]{1,0:T(8,128)S(1)}, f32[64,128]{1,0:T(8,128)}, u32[]{:S(2)}) copy-start(f32[64,128]{1,0:T(8,128)} %constant.23.clone.twist_sin_ref) | copy-start | bytes 98308
  4.2 48.9 %copy-start.5 = (f32[64,128]{1,0:T(8,128)S(1)}, f32[64,128]{1,0:T(8,128)}, u32[]{:S(2)}) copy-start(f32[64,128]{1,0:T(8,128)} %constant.22.clone.twist_cos_ref) | copy-start | bytes 98308
  4.2 48.9 %copy-start.6 = (bf16[128,64]{1,0:T(8,128)(2,1)S(1)}, bf16[128,64]{1,0:T(8,128)(2,1)}, u32[]{:S(2)}) copy-start(bf16[128,64]{1,0:T(8,128)(2,1)} %constant.17.clone.first_taps_ref) | copy-start | bytes 49156
  4.2 48.9 %copy-start.7 = (bf16[64,128]{1,0:T(8,128)(2,1)S(1)}, bf16[64,128]{1,0:T(8,128)(2,1)}, u32[]{:S(2)}) copy-start(bf16[64,128]{1,0:T(8,128)(2,1)} %constant.21.clone.last_taps_ref) | copy-start | bytes 49156
  107.0 2.3 %collective-permute-start = (bf16[32,48,128]{2,1,0:T(8,128)(2,1)S(1)}, bf16[32,48,128]{2,1,0:T(8,128)(2,1)S(1)}, u32[]{:S(2)}, u32[]{:S(2)}) collective-permute-start(bf16[32,48,128]{2,1,0:T(8,128)(2,1)S(1)} %slice.4.own_ref), channel_id=1, source_target_pairs={{0,1},{1,0},{2,3},{3,2},{4,5},{5,4},{6,7},{7,6},{8,9},{9,8},{10,11... | collective-permute-start | bytes 1179656 | tf_op jit(solution)/shard_map/ppermute | solution.py:388

commit v4 on v3

--- a/solution.py
+++ b/solution.py
@@ -363,8 +363,8 @@
             pltpu.VMEM((tokens, channels), jnp.bfloat16),
             pltpu.VMEM((tokens, channels), jnp.bfloat16),
             pltpu.VMEM((own * LANES, channels), jnp.bfloat16),
-            pltpu.VMEM((count * group * pair, LANES), jnp.float32),
-            pltpu.VMEM((count * group * own, LANES), jnp.float32),
+            pltpu.VMEM(((count * group + 1) * pair, LANES), jnp.float32),
+            pltpu.VMEM(((count * group + 1) * own, LANES), jnp.float32),
             pltpu.SemaphoreType.DMA((5,)),
         ],
         compiler_params=LIMIT,
@@ -377,8 +377,8 @@
         in_specs=[VMEM] * 9,
         out_specs=VMEM,
         scratch_shapes=[
-            pltpu.VMEM((count * group * own, LANES), jnp.float32),
-            pltpu.VMEM((2 * blocks * group * half, LANES), jnp.float32),
+            pltpu.VMEM(((count + 1) * group * own, LANES), jnp.float32),
+            pltpu.VMEM(((2 * blocks + 1) * group * half, LANES), jnp.float32),
         ],
         compiler_params=LIMIT,
         name="spectral",
@@ -392,7 +392,7 @@
         in_specs=[SMEM, VMEM],
         out_specs=[HBM, HBM],
         scratch_shapes=[
-            pltpu.VMEM((count * group * pair, LANES), jnp.float32),
+            pltpu.VMEM(((count * group + 1) * pair, LANES), jnp.float32),
             pltpu.VMEM((tokens, channels), jnp.bfloat16),
             pltpu.VMEM((tokens, channels), jnp.bfloat16),
             pltpu.SemaphoreType.DMA((2 * rows,)),
@@ -406,7 +406,7 @@
         in_specs=[VMEM, VMEM],
         out_specs=HBM,
         scratch_shapes=[
-            pltpu.VMEM((2 * count * group * half, LANES), jnp.float32),
+            pltpu.VMEM(((2 * count * group + 1) * half, LANES), jnp.float32),
             pltpu.VMEM((tokens, channels), jnp.bfloat16),
             pltpu.SemaphoreType.DMA((2 * half,)),
         ],

time: 111 us -> 111 us (level)
  no operation moved by 1% of the time
where the time goes in v4:
time: 111 us; the launch traced here: 110 us
  blocking collectives  98.1 us (88%)
  Pallas kernels  10.7 us (10%)
  between operations  1.43 us (1%)
    all_to_all x1, blocking collectives, per_device(): lax.all_to_all(results, everyone, split_axis=0, concat_axis=0, tiled=True)  49.3 us
    all_to_all x1, blocking collectives, per_device(): lax.all_to_all(packed, everyone, split_axis=0, concat_axis=0, tiled=True)  48.8 us
    pallas_call x1, Pallas kernels, per_device(): pl.pallas_call(functools.partial(spectral_kernel, blocks, rows, replicas,...  4.58 us
    pallas_call x1, Pallas kernels, per_device(): pl.pallas_call(functools.partial(pack_kernel, own, group, count), out_sha...  2.82 us
  transfers between devices with their start and end apart: 1, of which 0 were waited for; matrix products, arithmetic and copies ran while one was open for 0% of the time, Pallas kernels for 2%

profile of v4, /device:TPU:0, one launch (start us, length us, event | category | flops | bytes accessed | tf_op | source)
XLA Modules:
  0.0 110.4 jit_solution(15900187981306284314)
XLA Ops:
  1.3 2.8 %pack.1 = bf16[32,216,128]{2,1,0:T(8,128)(2,1)S(1)} custom-call(s32[1,1]{1,0:T(1,128)S(6)} %copy.15.mask_ref, bf16[1,1024,384]{2,1,0:T(8,128)(2,1)} %signal_ref.1, bf16[1,1024,384]{2,1,0:T(8,128)(2,1)} %grad_ref.1, bf16[1024,384]{1,0:T(8,128)(2,1)} %filter_ref.1), custom_call_target="tpu_custom_call" | custom-call | tf_op jit(solution)/shard_map/pack/pallas_call | solution.py:357
  4.1 0.0 copy-start
  4.1 0.0 copy-start.1
  4.1 0.0 copy-start.2
  4.1 0.0 copy-start.3
  4.2 0.0 copy-start.4
  4.2 0.0 copy-start.5
  4.2 0.0 copy-start.6
  4.2 0.0 copy-start.7
  4.2 48.8 %all_to_all.10.recv_ref = bf16[32,216,128]{2,1,0:T(8,128)(2,1)S(1)} all-to-all(bf16[32,216,128]{2,1,0:T(8,128)(2,1)S(1)} %pack.1), channel_id=1, replica_groups=mesh['seq'=8,'dp'=4] {'seq','dp'}, dimensions={0} | all-to-all | bytes 3538944 | tf_op jit(solution)/shard_map/all_to_all | solution.py:373
  53.0 0.0 copy-done
  53.0 0.0 copy-done.1
  53.0 0.0 copy-done.2
  53.0 0.0 copy-done.3
  53.0 0.0 copy-done.4
  53.0 0.0 copy-done.5
  53.0 0.0 copy-done.6
  53.0 0.0 copy-done.7
  53.1 4.6 %spectral.1 = bf16[32,240,128]{2,1,0:T(8,128)(2,1)S(1)} custom-call(bf16[32,216,128]{2,1,0:T(8,128)(2,1)S(1)} %all_to_all.10.recv_ref, bf16[256,128]{1,0:T(8,128)(2,1)S(1)} %copy-done.3, bf16[128,64]{1,0:T(8,128)(2,1)S(1)} %copy-done.6, bf16[256,256]{1,0:T(8,128)(2,1)S(1)} %copy-done.1, bf16[256,256]{1,0:T(8,128)(2,1)S(1)} %copy-done, ...), custom_call_target="tpu_custom_call" | custom-call | tf_op jit(solution)/shard_map/spectral/pallas_call | solution.py:374
  57.6 49.3 %all_to_all.11.recv_ref = bf16[32,240,128]{2,1,0:T(8,128)(2,1)S(1)} all-to-all(bf16[32,240,128]{2,1,0:T(8,128)(2,1)S(1)} %spectral.1), channel_id=1, replica_groups=mesh['seq'=8,'dp'=4] {'seq','dp'}, dimensions={0} | all-to-all | bytes 3932160 | tf_op jit(solution)/shard_map/all_to_all | solution.py:386
  107.0 0.1 collective-permute-start
  107.1 2.2 %unpack.1 = (bf16[1,1024,384]{2,1,0:T(8,128)(2,1)}, bf16[1,1024,384]{2,1,0:T(8,128)(2,1)}) custom-call(s32[1,1]{1,0:T(1,128)S(6)} %copy.15.mask_ref, bf16[32,240,128]{2,1,0:T(8,128)(2,1)S(1)} %all_to_all.11.recv_ref), custom_call_target="tpu_custom_call" | custom-call | tf_op jit(solution)/shard_map/unpack/pallas_call | solution.py:389
  109.3 0.0 collective-permute-done.other_ref
  109.3 1.1 unpack_taps.1
  (1 shorter events, 0.0 us)
Async XLA Ops:
  4.1 48.9 %copy-start = (bf16[256,256]{1,0:T(8,128)(2,1)S(1)}, bf16[256,256]{1,0:T(8,128)(2,1)}, u32[]{:S(2)}) copy-start(bf16[256,256]{1,0:T(8,128)(2,1)} %constant.19.clone.inner_back_ref) | copy-start | bytes 393220
  4.1 48.9 %copy-start.1 = (bf16[256,256]{1,0:T(8,128)(2,1)S(1)}, bf16[256,256]{1,0:T(8,128)(2,1)}, u32[]{:S(2)}) copy-start(bf16[256,256]{1,0:T(8,128)(2,1)} %constant.18.clone.inner_ref) | copy-start | bytes 393220
  4.1 48.9 %copy-start.2 = (bf16[128,256]{1,0:T(8,128)(2,1)S(1)}, bf16[128,256]{1,0:T(8,128)(2,1)}, u32[]{:S(2)}) copy-start(bf16[128,256]{1,0:T(8,128)(2,1)} %constant.20.clone.last_ref) | copy-start | bytes 196612
  4.1 48.9 %copy-start.3 = (bf16[256,128]{1,0:T(8,128)(2,1)S(1)}, bf16[256,128]{1,0:T(8,128)(2,1)}, u32[]{:S(2)}) copy-start(bf16[256,128]{1,0:T(8,128)(2,1)} %constant.16.clone.first_ref) | copy-start | bytes 196612
  4.2 48.9 %copy-start.4 = (f32[64,128]{1,0:T(8,128)S(1)}, f32[64,128]{1,0:T(8,128)}, u32[]{:S(2)}) copy-start(f32[64,128]{1,0:T(8,128)} %constant.23.clone.twist_sin_ref) | copy-start | bytes 98308
  4.2 48.9 %copy-start.5 = (f32[64,128]{1,0:T(8,128)S(1)}, f32[64,128]{1,0:T(8,128)}, u32[]{:S(2)}) copy-start(f32[64,128]{1,0:T(8,128)} %constant.22.clone.twist_cos_ref) | copy-start | bytes 98308
  4.2 48.9 %copy-start.6 = (bf16[128,64]{1,0:T(8,128)(2,1)S(1)}, bf16[128,64]{1,0:T(8,128)(2,1)}, u32[]{:S(2)}) copy-start(bf16[128,64]{1,0:T(8,128)(2,1)} %constant.17.clone.first_taps_ref) | copy-start | bytes 49156
  4.2 48.9 %copy-start.7 = (bf16[64,128]{1,0:T(8,128)(2,1)S(1)}, bf16[64,128]{1,0:T(8,128)(2,1)}, u32[]{:S(2)}) copy-start(bf16[64,128]{1,0:T(8,128)(2,1)} %constant.21.clone.last_taps_ref) | copy-start | bytes 49156
  107.0 2.3 %collective-permute-start = (bf16[32,48,128]{2,1,0:T(8,128)(2,1)S(1)}, bf16[32,48,128]{2,1,0:T(8,128)(2,1)S(1)}, u32[]{:S(2)}, u32[]{:S(2)}) collective-permute-start(bf16[32,48,128]{2,1,0:T(8,128)(2,1)S(1)} %slice.4.own_ref), channel_id=1, source_target_pairs={{0,1},{1,0},{2,3},{3,2},{4,5},{5,4},{6,7},{7,6},{8,9},{9,8},{10,11... | collective-permute-start | bytes 1179656 | tf_op jit(solution)/shard_map/ppermute | solution.py:388

commit v5 on v4

--- a/solution.py
+++ b/solution.py
@@ -12,6 +12,7 @@
 
 LANES = 128
 BLK = 1024
+PAD = 1
 BF16 = ml_dtypes.bfloat16
 
 
@@ -73,6 +74,7 @@
     tokens, channels = filter_ref.shape
     rows = tokens // LANES
     pair = 2 * rows
+    pitch = pair + PAD
     block_rows = BLK // LANES
     parts = in_sems.shape[0] // 2
     part_rows = rows // parts
@@ -109,18 +111,22 @@
         copies[2 * part].wait()
         for row in places:
             keep = mask_ref[0, row // block_rows].astype(jnp.float32)
-            pair_scr[pl.ds(row, channels, stride=pair), :] = (
+            pair_scr[pl.ds(row, channels, stride=pitch), :] = (
                 signal_buf[row * LANES : (row + 1) * LANES, :].astype(jnp.float32).T * keep
             )
         copies[2 * part + 1].wait()
         for row in places:
-            pair_scr[pl.ds(rows + row, channels, stride=pair), :] = (
+            pair_scr[pl.ds(rows + row, channels, stride=pitch), :] = (
                 grad_buf[row * LANES : (row + 1) * LANES, :].astype(jnp.float32).T
             )
     for target in range(count):
-        send_ref[target, : group * pair, :] = pair_scr[
-            target * group * pair : (target + 1) * group * pair, :
-        ].astype(jnp.bfloat16)
+        send_ref[target, : group * pair, :] = jnp.concatenate(
+            [
+                pair_scr[index * pitch : index * pitch + pair, :]
+                for index in range(target * group, (target + 1) * group)
+            ],
+            axis=0,
+        ).astype(jnp.bfloat16)
         send_ref[target, group * pair :, :] = tap_scr[
             target * group * own : (target + 1) * group * own, :
         ].astype(jnp.bfloat16)
@@ -136,10 +142,10 @@
     pair = 2 * rows
     own = rows // replicas
     half = rows // 2
-    tap_rows = group * own
-    back_rows = group * half
+    tap_rows = group * own + PAD
+    back_rows = group * half + PAD
     for source in range(count):
-        tap_scr[source * tap_rows : (source + 1) * tap_rows, :] = recv_ref[
+        tap_scr[source * tap_rows : source * tap_rows + group * own, :] = recv_ref[
             source, group * pair :, :
         ].astype(jnp.float32)
 
@@ -265,7 +271,7 @@
     for target in range(count):
         place = target % replicas % 2 * blocks + target // replicas
         send_ref[target, group * pair :, :] = back_scr[
-            place * back_rows : (place + 1) * back_rows, :
+            place * back_rows : place * back_rows + group * half, :
         ].astype(jnp.bfloat16)
 
 
@@ -275,23 +281,25 @@
     tokens, channels = conv_ref.shape[1:]
     rows = tokens // LANES
     pair = 2 * rows
+    pitch = pair + PAD
     block_rows = BLK // LANES
     size = group * pair
     for source in range(recv_ref.shape[0]):
-        pair_scr[source * size : (source + 1) * size, :] = recv_ref[source, :size, :].astype(
-            jnp.float32
-        )
+        whole = recv_ref[source, :size, :].astype(jnp.float32)
+        for index in range(group):
+            start = (source * group + index) * pitch
+            pair_scr[start : start + pair, :] = whole[index * pair : (index + 1) * pair]
     copies = []
     for row in range(rows):
         span = pl.ds(row * LANES, LANES)
         keep = mask_ref[0, row // block_rows].astype(jnp.float32)
-        conv_buf[span, :] = pair_scr[pl.ds(row, channels, stride=pair), :].T.astype(jnp.bfloat16)
+        conv_buf[span, :] = pair_scr[pl.ds(row, channels, stride=pitch), :].T.astype(jnp.bfloat16)
         copies.append(
             pltpu.make_async_copy(conv_buf.at[span, :], conv_ref.at[0, span, :], sems.at[2 * row])
         )
         copies[-1].start()
         grad_buf[span, :] = (
-            pair_scr[pl.ds(rows + row, channels, stride=pair), :].T * keep
+            pair_scr[pl.ds(rows + row, channels, stride=pitch), :].T * keep
         ).astype(jnp.bfloat16)
         copies.append(
             pltpu.make_async_copy(
@@ -363,7 +371,7 @@
             pltpu.VMEM((tokens, channels), jnp.bfloat16),
             pltpu.VMEM((tokens, channels), jnp.bfloat16),
             pltpu.VMEM((own * LANES, channels), jnp.bfloat16),
-            pltpu.VMEM(((count * group + 1) * pair, LANES), jnp.float32),
+            pltpu.VMEM(((count * group + 1) * (pair + PAD), LANES), jnp.float32),
             pltpu.VMEM(((count * group + 1) * own, LANES), jnp.float32),
             pltpu.SemaphoreType.DMA((5,)),
         ],
@@ -377,8 +385,8 @@
         in_specs=[VMEM] * 9,
         out_specs=VMEM,
         scratch_shapes=[
-            pltpu.VMEM(((count + 1) * group * own, LANES), jnp.float32),
-            pltpu.VMEM(((2 * blocks + 1) * group * half, LANES), jnp.float32),
+            pltpu.VMEM(((count + 1) * (group * own + PAD), LANES), jnp.float32),
+            pltpu.VMEM(((2 * blocks + 1) * (group * half + PAD), LANES), jnp.float32),
         ],
         compiler_params=LIMIT,
         name="spectral",
@@ -392,7 +400,7 @@
         in_specs=[SMEM, VMEM],
         out_specs=[HBM, HBM],
         scratch_shapes=[
-            pltpu.VMEM(((count * group + 1) * pair, LANES), jnp.float32),
+            pltpu.VMEM(((count * group + 1) * (pair + PAD), LANES), jnp.float32),
             pltpu.VMEM((tokens, channels), jnp.bfloat16),
             pltpu.VMEM((tokens, channels), jnp.bfloat16),
             pltpu.SemaphoreType.DMA((2 * rows,)),

time: 111 us -> 109 us (0.982)
  Pallas kernels: 10.7 us -> 9.16 us
  transfers between devices with their start and end apart: 1 -> 1, of which waited for: 0 -> 1; matrix products, arithmetic and copies ran while one was open for 0% -> 0% of each run, Pallas kernels for 2% -> 1%
where the time goes in v5:
time: 109 us
  blocking collectives  98.1 us (90%)
  Pallas kernels  9.16 us (8%)
  between operations  1.42 us (1%)
    all_to_all x1, blocking collectives, per_device(): lax.all_to_all(results, everyone, split_axis=0, concat_axis=0, tiled=True)  49.3 us
    all_to_all x1, blocking collectives, per_device(): lax.all_to_all(packed, everyone, split_axis=0, concat_axis=0, tiled=True)  48.8 us
    pallas_call x1, Pallas kernels, per_device(): pl.pallas_call(functools.partial(spectral_kernel, blocks, rows, replicas,...  4.45 us
  transfers between devices with their start and end apart: 1, of which 1 were waited for; matrix products, arithmetic and copies ran while one was open for 0% of the time, Pallas kernels for 1%

profile of v5, /device:TPU:0, one launch (start us, length us, event | category | flops | bytes accessed | tf_op | source)
XLA Modules:
  0.0 108.9 jit_solution(3597820901275309003)
XLA Ops:
  1.3 2.0 %pack.1 = bf16[32,216,128]{2,1,0:T(8,128)(2,1)S(1)} custom-call(s32[1,1]{1,0:T(1,128)S(6)} %copy.15.mask_ref, bf16[1,1024,384]{2,1,0:T(8,128)(2,1)} %signal_ref.1, bf16[1,1024,384]{2,1,0:T(8,128)(2,1)} %grad_ref.1, bf16[1024,384]{1,0:T(8,128)(2,1)} %filter_ref.1), custom_call_target="tpu_custom_call" | custom-call | tf_op jit(solution)/shard_map/pack/pallas_call | solution.py:365
  3.3 0.0 copy-start
  3.3 0.0 copy-start.1
  3.3 0.0 copy-start.2
  3.3 0.0 copy-start.3
  3.3 0.0 copy-start.4
  3.3 0.0 copy-start.5
  3.4 0.0 copy-start.6
  3.4 0.0 copy-start.7
  3.4 48.8 %all_to_all.10.recv_ref = bf16[32,216,128]{2,1,0:T(8,128)(2,1)S(1)} all-to-all(bf16[32,216,128]{2,1,0:T(8,128)(2,1)S(1)} %pack.1), channel_id=1, replica_groups=mesh['seq'=8,'dp'=4] {'seq','dp'}, dimensions={0} | all-to-all | bytes 3538944 | tf_op jit(solution)/shard_map/all_to_all | solution.py:381
  52.2 0.0 copy-done
  52.2 0.0 copy-done.1
  52.2 0.0 copy-done.2
  52.2 0.0 copy-done.3
  52.2 0.0 copy-done.4
  52.2 0.0 copy-done.5
  52.2 0.0 copy-done.6
  52.2 0.0 copy-done.7
  52.2 4.5 %spectral.1 = bf16[32,240,128]{2,1,0:T(8,128)(2,1)S(1)} custom-call(bf16[32,216,128]{2,1,0:T(8,128)(2,1)S(1)} %all_to_all.10.recv_ref, bf16[256,128]{1,0:T(8,128)(2,1)S(1)} %copy-done.3, bf16[128,64]{1,0:T(8,128)(2,1)S(1)} %copy-done.6, bf16[256,256]{1,0:T(8,128)(2,1)S(1)} %copy-done.1, bf16[256,256]{1,0:T(8,128)(2,1)S(1)} %copy-done, ...), custom_call_target="tpu_custom_call" | custom-call | tf_op jit(solution)/shard_map/spectral/pallas_call | solution.py:382
  56.7 49.3 %all_to_all.11.recv_ref = bf16[32,240,128]{2,1,0:T(8,128)(2,1)S(1)} all-to-all(bf16[32,240,128]{2,1,0:T(8,128)(2,1)S(1)} %spectral.1), channel_id=1, replica_groups=mesh['seq'=8,'dp'=4] {'seq','dp'}, dimensions={0} | all-to-all | bytes 3932160 | tf_op jit(solution)/shard_map/all_to_all | solution.py:394
  106.1 0.1 collective-permute-start
  106.1 1.6 %unpack.1 = (bf16[1,1024,384]{2,1,0:T(8,128)(2,1)}, bf16[1,1024,384]{2,1,0:T(8,128)(2,1)}) custom-call(s32[1,1]{1,0:T(1,128)S(6)} %copy.15.mask_ref, bf16[32,240,128]{2,1,0:T(8,128)(2,1)S(1)} %all_to_all.11.recv_ref), custom_call_target="tpu_custom_call" | custom-call | tf_op jit(solution)/shard_map/unpack/pallas_call | solution.py:397
  107.8 0.1 collective-permute-done.other_ref
  107.8 1.1 unpack_taps.1
  (1 shorter events, 0.0 us)
Async XLA Ops:
  3.3 48.9 %copy-start = (bf16[256,256]{1,0:T(8,128)(2,1)S(1)}, bf16[256,256]{1,0:T(8,128)(2,1)}, u32[]{:S(2)}) copy-start(bf16[256,256]{1,0:T(8,128)(2,1)} %constant.19.clone.inner_back_ref) | copy-start | bytes 393220
  3.3 48.9 %copy-start.1 = (bf16[256,256]{1,0:T(8,128)(2,1)S(1)}, bf16[256,256]{1,0:T(8,128)(2,1)}, u32[]{:S(2)}) copy-start(bf16[256,256]{1,0:T(8,128)(2,1)} %constant.18.clone.inner_ref) | copy-start | bytes 393220
  3.3 48.9 %copy-start.2 = (bf16[128,256]{1,0:T(8,128)(2,1)S(1)}, bf16[128,256]{1,0:T(8,128)(2,1)}, u32[]{:S(2)}) copy-start(bf16[128,256]{1,0:T(8,128)(2,1)} %constant.20.clone.last_ref) | copy-start | bytes 196612
  3.3 48.9 %copy-start.3 = (bf16[256,128]{1,0:T(8,128)(2,1)S(1)}, bf16[256,128]{1,0:T(8,128)(2,1)}, u32[]{:S(2)}) copy-start(bf16[256,128]{1,0:T(8,128)(2,1)} %constant.16.clone.first_ref) | copy-start | bytes 196612
  3.3 48.9 %copy-start.4 = (f32[64,128]{1,0:T(8,128)S(1)}, f32[64,128]{1,0:T(8,128)}, u32[]{:S(2)}) copy-start(f32[64,128]{1,0:T(8,128)} %constant.23.clone.twist_sin_ref) | copy-start | bytes 98308
  3.3 48.9 %copy-start.5 = (f32[64,128]{1,0:T(8,128)S(1)}, f32[64,128]{1,0:T(8,128)}, u32[]{:S(2)}) copy-start(f32[64,128]{1,0:T(8,128)} %constant.22.clone.twist_cos_ref) | copy-start | bytes 98308
  3.4 48.9 %copy-start.6 = (bf16[128,64]{1,0:T(8,128)(2,1)S(1)}, bf16[128,64]{1,0:T(8,128)(2,1)}, u32[]{:S(2)}) copy-start(bf16[128,64]{1,0:T(8,128)(2,1)} %constant.17.clone.first_taps_ref) | copy-start | bytes 49156
  3.4 48.9 %copy-start.7 = (bf16[64,128]{1,0:T(8,128)(2,1)S(1)}, bf16[64,128]{1,0:T(8,128)(2,1)}, u32[]{:S(2)}) copy-start(bf16[64,128]{1,0:T(8,128)(2,1)} %constant.21.clone.last_taps_ref) | copy-start | bytes 49156
  106.1 1.8 %collective-permute-start = (bf16[32,48,128]{2,1,0:T(8,128)(2,1)S(1)}, bf16[32,48,128]{2,1,0:T(8,128)(2,1)S(1)}, u32[]{:S(2)}, u32[]{:S(2)}) collective-permute-start(bf16[32,48,128]{2,1,0:T(8,128)(2,1)S(1)} %slice.4.own_ref), channel_id=1, source_target_pairs={{0,1},{1,0},{2,3},{3,2},{4,5},{5,4},{6,7},{7,6},{8,9},{9,8},{10,11... | collective-permute-start | bytes 1179656 | tf_op jit(solution)/shard_map/ppermute | solution.py:396

commit v6 on v5

--- a/solution.py
+++ b/solution.py
@@ -19,6 +19,13 @@
 def wave(product, period):
     angle = 2.0 * np.pi / period * (product % period)
     return np.cos(angle), np.sin(angle)
+
+
+def slot_order(blocks, replicas):
+    turns = [0] + list(range((blocks - 1) // 2, 0, -1))
+    return [
+        (2 * turn + odd, seq) for odd in range(2) for seq in range(replicas) for turn in turns
+    ]
 
 
 def make_tables(blocks, rows, replicas):
@@ -37,11 +44,8 @@
         first[which, 1, :, :, which, :] = -sin_a[:, plain]
         last[:, which, :, which, 0, :] = np.moveaxis(cos_a[:, plain], 0, 2)
         last[:, which, :, which, 1, :] = -np.moveaxis(sin_a[:, plain], 0, 2)
-    taps = (
-        np.arange(own)[:, None, None]
-        + rows * np.arange(blocks)[None, :, None]
-        + own * np.arange(replicas)[None, None, :]
-    ).reshape(-1)
+    starts = np.array([rows * block + own * seq for block, seq in slot_order(blocks, replicas)])
+    taps = (np.arange(own)[:, None] + starts[None, :]).reshape(-1)
     first_taps = np.concatenate([cos_a[:, taps], -sin_a[:, taps]], axis=0)
     back = (
         np.arange(half)[:, None, None]
@@ -95,30 +99,28 @@
                 grad_ref.at[0, span, :], grad_buf.at[span, :], in_sems.at[2 * part + 1]
             )
         )
-    filter_copy.start()
     for copy in copies:
         copy.start()
+    filter_copy.start()
     if group * count != channels:
         pair_scr[...] = jnp.zeros_like(pair_scr)
         tap_scr[...] = jnp.zeros_like(tap_scr)
+    copies[0].wait()
+    for row in range(rows):
+        keep = mask_ref[0, row // block_rows].astype(jnp.float32)
+        pair_scr[pl.ds(row, channels, stride=pitch), :] = (
+            signal_buf[row * LANES : (row + 1) * LANES, :].astype(jnp.float32).T * keep
+        )
+    copies[1].wait()
     filter_copy.wait()
+    for row in range(rows):
+        pair_scr[pl.ds(rows + row, channels, stride=pitch), :] = (
+            grad_buf[row * LANES : (row + 1) * LANES, :].astype(jnp.float32).T
+        )
     for row in range(own):
         tap_scr[pl.ds(row, channels, stride=own), :] = (
             filter_buf[row * LANES : (row + 1) * LANES, :].astype(jnp.float32).T
         )
-    for part in range(parts):
-        places = range(part * part_rows, (part + 1) * part_rows)
-        copies[2 * part].wait()
-        for row in places:
-            keep = mask_ref[0, row // block_rows].astype(jnp.float32)
-            pair_scr[pl.ds(row, channels, stride=pitch), :] = (
-                signal_buf[row * LANES : (row + 1) * LANES, :].astype(jnp.float32).T * keep
-            )
-        copies[2 * part + 1].wait()
-        for row in places:
-            pair_scr[pl.ds(rows + row, channels, stride=pitch), :] = (
-                grad_buf[row * LANES : (row + 1) * LANES, :].astype(jnp.float32).T
-            )
     for target in range(count):
         send_ref[target, : group * pair, :] = jnp.concatenate(
             [
@@ -142,6 +144,7 @@
     pair = 2 * rows
     own = rows // replicas
     half = rows // 2
+    slots = {place: slot for slot, place in enumerate(slot_order(blocks, replicas))}
     tap_rows = group * own + PAD
     back_rows = group * half + PAD
     for source in range(count):
@@ -171,7 +174,7 @@
             [
                 jnp.concatenate(
                     [
-                        recv_ref[block * replicas + seq, pl.ds(offset, pair), :]
+                        recv_ref[slots[block, seq], pl.ds(offset, pair), :]
                         for block in range(blocks)
                     ],
                     axis=0,
@@ -249,7 +252,7 @@
         result = (dot(last_ref[...], columns) * factor).astype(jnp.bfloat16)
         for seq in range(replicas):
             for block in range(blocks):
-                send_ref[block * replicas + seq, pl.ds(offset, pair), :] = result[
+                send_ref[slots[block, seq], pl.ds(offset, pair), :] = result[
                     block * pair : (block + 1) * pair, seq * LANES : (seq + 1) * LANES
                 ]
         weights = dot(last_taps_ref[...], weight_column) * factor
@@ -268,8 +271,8 @@
             products[step - 1] = multiply(turned.pop(step - 1))
         if step < group:
             turned[step] = spread(step)
-    for target in range(count):
-        place = target % replicas % 2 * blocks + target // replicas
+    for (block, seq), target in slots.items():
+        place = seq % 2 * blocks + block
         send_ref[target, group * pair :, :] = back_scr[
             place * back_rows : place * back_rows + group * half, :
         ].astype(jnp.bfloat16)
@@ -359,6 +362,7 @@
     coarse = total // LANES
     factor = 1.0 / (total * math.sqrt(total))
     everyone = ("seq", "dp")
+    ring = [[block * replicas + seq for block, seq in slot_order(blocks, replicas)]]
     tables = [jnp.asarray(t) for t in make_tables(blocks, rows, replicas)]
 
     inputs = (signal, cotangent, filter_raw)
@@ -373,12 +377,12 @@
             pltpu.VMEM((own * LANES, channels), jnp.bfloat16),
             pltpu.VMEM(((count * group + 1) * (pair + PAD), LANES), jnp.float32),
             pltpu.VMEM(((count * group + 1) * own, LANES), jnp.float32),
-            pltpu.SemaphoreType.DMA((5,)),
+            pltpu.SemaphoreType.DMA((3,)),
         ],
         compiler_params=LIMIT,
         name="pack",
     )(block_mask, *(pltpu.with_memory_space_constraint(x, pltpu.HBM) for x in inputs))
-    received = lax.all_to_all(packed, everyone, split_axis=0, concat_axis=0, tiled=True)
+    received = lax.all_to_all(packed, everyone, split_axis=0, concat_axis=0, tiled=True, axis_index_groups=ring)
     results = pl.pallas_call(
         functools.partial(spectral_kernel, blocks, rows, replicas, group, factor),
         out_shape=jax.ShapeDtypeStruct((count, group * (pair + half), LANES), jnp.bfloat16),
@@ -391,7 +395,7 @@
         compiler_params=LIMIT,
         name="spectral",
     )(received, *tables)
-    returned = lax.all_to_all(results, everyone, split_axis=0, concat_axis=0, tiled=True)
+    returned = lax.all_to_all(results, everyone, split_axis=0, concat_axis=0, tiled=True, axis_index_groups=ring)
     own_taps = returned[:, group * pair :, :]
     other_taps = lax.ppermute(own_taps, "dp", [(i, i ^ 1) for i in range(replicas)])
     conv_out, signal_grad = pl.pallas_call(

time: 109 us -> 109 us (level)
  blocking collectives: 98.1 us -> 96.3 us
  starting transfers between devices: 0.07 us -> 1.57 us
    all_to_all x2, blocking collectives: 98.1 us -> 96.3 us  [the longest x1 48.5 us: per_device(): lax.all_to_all(results, everyone, split_axis=0, concat_axis=0, tiled=True...]
    ppermute x1, starting transfers between devices: 0.07 us -> 1.57 us  [per_device(): lax.ppermute(own_taps, 'dp', [(i, i ^ 1) for i in range(replicas)])]
  transfers between devices with their start and end apart: 1 -> 1, of which waited for: 1 -> 0; matrix products, arithmetic and copies ran while one was open for 0% -> 0% of each run, Pallas kernels for 1% -> 1%
where the time goes in v6:
time: 109 us; the launch traced here: 108 us
  blocking collectives  96.3 us (88%)
  Pallas kernels  9.05 us (8%)
  starting transfers between devices  1.57 us (1%)
  between operations  1.42 us (1%)
    all_to_all x1, blocking collectives, per_device(): lax.all_to_all(results, everyone, split_axis=0, concat_axis=0, tiled=True...  48.5 us
    all_to_all x1, blocking collectives, per_device(): lax.all_to_all(packed, everyone, split_axis=0, concat_axis=0, tiled=True,...  47.8 us
    pallas_call x1, Pallas kernels, per_device(): pl.pallas_call(functools.partial(spectral_kernel, blocks, rows, replicas,...  4.45 us
  transfers between devices with their start and end apart: 1, of which 0 were waited for; matrix products, arithmetic and copies ran while one was open for 0% of the time, Pallas kernels for 1%

profile of v6, /device:TPU:0, one launch (start us, length us, event | category | flops | bytes accessed | tf_op | source)
XLA Modules:
  0.0 108.5 jit_solution(14667061757019496139)
XLA Ops:
  1.3 1.9 %pack.1 = bf16[32,216,128]{2,1,0:T(8,128)(2,1)S(1)} custom-call(s32[1,1]{1,0:T(1,128)S(6)} %copy.15.mask_ref, bf16[1,1024,384]{2,1,0:T(8,128)(2,1)} %signal_ref.1, bf16[1,1024,384]{2,1,0:T(8,128)(2,1)} %grad_ref.1, bf16[1024,384]{1,0:T(8,128)(2,1)} %filter_ref.1), custom_call_target="tpu_custom_call" | custom-call | tf_op jit(solution)/shard_map/pack/pallas_call | solution.py:369
  3.2 0.0 copy-start
  3.2 0.0 copy-start.1
  3.2 0.0 copy-start.2
  3.2 0.0 copy-start.3
  3.2 0.0 copy-start.4
  3.2 0.0 copy-start.5
  3.3 0.0 copy-start.6
  3.3 0.0 copy-start.7
  3.3 47.8 %all_to_all.10.recv_ref = bf16[32,216,128]{2,1,0:T(8,128)(2,1)S(1)} all-to-all(bf16[32,216,128]{2,1,0:T(8,128)(2,1)S(1)} %pack.1), channel_id=1, replica_groups={{0,24,16,8,1,25,17,9,2,26,18,10,3,27,19,11,4,28,20,12,5,29,21,13,6,30,2..., dimensions={0} | all-to-all | bytes 3538944 | tf_op jit(solution)/shard_map/all_to_all | solution.py:385
  51.1 0.0 copy-done
  51.1 0.0 copy-done.1
  51.1 0.0 copy-done.2
  51.1 0.0 copy-done.3
  51.1 0.0 copy-done.4
  51.1 0.0 copy-done.5
  51.2 0.0 copy-done.6
  51.2 0.0 copy-done.7
  51.2 4.4 %spectral.1 = bf16[32,240,128]{2,1,0:T(8,128)(2,1)S(1)} custom-call(bf16[32,216,128]{2,1,0:T(8,128)(2,1)S(1)} %all_to_all.10.recv_ref, bf16[256,128]{1,0:T(8,128)(2,1)S(1)} %copy-done.3, bf16[128,64]{1,0:T(8,128)(2,1)S(1)} %copy-done.6, bf16[256,256]{1,0:T(8,128)(2,1)S(1)} %copy-done.1, bf16[256,256]{1,0:T(8,128)(2,1)S(1)} %copy-done, ...), custom_call_target="tpu_custom_call" | custom-call | tf_op jit(solution)/shard_map/spectral/pallas_call | solution.py:386
  55.6 48.5 %all_to_all.11.recv_ref = bf16[32,240,128]{2,1,0:T(8,128)(2,1)S(1)} all-to-all(bf16[32,240,128]{2,1,0:T(8,128)(2,1)S(1)} %spectral.1), channel_id=1, replica_groups={{0,24,16,8,1,25,17,9,2,26,18,10,3,27,19,11,4,28,20,12,5,29,21,13,6,30,2..., dimensions={0} | all-to-all | bytes 3932160 | tf_op jit(solution)/shard_map/all_to_all | solution.py:398
  104.2 1.6 %collective-permute-start = (bf16[32,48,128]{2,1,0:T(8,128)(2,1)S(1)}, bf16[32,48,128]{2,1,0:T(8,128)(2,1)S(1)}, u32[]{:S(2)}, u32[]{:S(2)}) collective-permute-start(bf16[32,48,128]{2,1,0:T(8,128)(2,1)S(1)} %slice.4.own_ref), channel_id=1, source_target_pairs={{0,1},{1,0},{2,3},{3,2},{4,5},{5,4},{6,7},{7,6},{8,9},{9,8},{10,11... | collective-permute-start | bytes 1179656 | tf_op jit(solution)/shard_map/ppermute | solution.py:400
  105.8 1.6 %unpack.1 = (bf16[1,1024,384]{2,1,0:T(8,128)(2,1)}, bf16[1,1024,384]{2,1,0:T(8,128)(2,1)}) custom-call(s32[1,1]{1,0:T(1,128)S(6)} %copy.15.mask_ref, bf16[32,240,128]{2,1,0:T(8,128)(2,1)S(1)} %all_to_all.11.recv_ref), custom_call_target="tpu_custom_call" | custom-call | tf_op jit(solution)/shard_map/unpack/pallas_call | solution.py:401
  107.4 0.0 collective-permute-done.other_ref
  107.4 1.1 %unpack_taps.1 = bf16[1024,384]{1,0:T(8,128)(2,1)} custom-call(bf16[32,48,128]{2,1,0:T(8,128)(2,1)S(1)} %slice.4.own_ref, bf16[32,48,128]{2,1,0:T(8,128)(2,1)S(1)} %collective-permute-done.other_ref), custom_call_target="tpu_custom_call" | custom-call | tf_op jit(solution)/shard_map/unpack_taps/pallas_call | solution.py:415
  (1 shorter events, 0.0 us)
Async XLA Ops:
  3.2 47.9 %copy-start = (bf16[256,256]{1,0:T(8,128)(2,1)S(1)}, bf16[256,256]{1,0:T(8,128)(2,1)}, u32[]{:S(2)}) copy-start(bf16[256,256]{1,0:T(8,128)(2,1)} %constant.19.clone.inner_back_ref) | copy-start | bytes 393220
  3.2 47.9 %copy-start.1 = (bf16[256,256]{1,0:T(8,128)(2,1)S(1)}, bf16[256,256]{1,0:T(8,128)(2,1)}, u32[]{:S(2)}) copy-start(bf16[256,256]{1,0:T(8,128)(2,1)} %constant.18.clone.inner_ref) | copy-start | bytes 393220
  3.2 47.9 %copy-start.2 = (bf16[128,256]{1,0:T(8,128)(2,1)S(1)}, bf16[128,256]{1,0:T(8,128)(2,1)}, u32[]{:S(2)}) copy-start(bf16[128,256]{1,0:T(8,128)(2,1)} %constant.20.clone.last_ref) | copy-start | bytes 196612
  3.2 47.9 %copy-start.3 = (bf16[256,128]{1,0:T(8,128)(2,1)S(1)}, bf16[256,128]{1,0:T(8,128)(2,1)}, u32[]{:S(2)}) copy-start(bf16[256,128]{1,0:T(8,128)(2,1)} %constant.16.clone.first_ref) | copy-start | bytes 196612
  3.2 47.9 %copy-start.4 = (f32[64,128]{1,0:T(8,128)S(1)}, f32[64,128]{1,0:T(8,128)}, u32[]{:S(2)}) copy-start(f32[64,128]{1,0:T(8,128)} %constant.23.clone.twist_sin_ref) | copy-start | bytes 98308
  3.2 47.9 %copy-start.5 = (f32[64,128]{1,0:T(8,128)S(1)}, f32[64,128]{1,0:T(8,128)}, u32[]{:S(2)}) copy-start(f32[64,128]{1,0:T(8,128)} %constant.22.clone.twist_cos_ref) | copy-start | bytes 98308
  3.3 47.9 %copy-start.6 = (bf16[128,64]{1,0:T(8,128)(2,1)S(1)}, bf16[128,64]{1,0:T(8,128)(2,1)}, u32[]{:S(2)}) copy-start(bf16[128,64]{1,0:T(8,128)(2,1)} %constant.17.clone.first_taps_ref) | copy-start | bytes 49156
  3.3 47.9 %copy-start.7 = (bf16[64,128]{1,0:T(8,128)(2,1)S(1)}, bf16[64,128]{1,0:T(8,128)(2,1)}, u32[]{:S(2)}) copy-start(bf16[64,128]{1,0:T(8,128)(2,1)} %constant.21.clone.last_taps_ref) | copy-start | bytes 49156
  104.2 3.2 %collective-permute-start = (bf16[32,48,128]{2,1,0:T(8,128)(2,1)S(1)}, bf16[32,48,128]{2,1,0:T(8,128)(2,1)S(1)}, u32[]{:S(2)}, u32[]{:S(2)}) collective-permute-start(bf16[32,48,128]{2,1,0:T(8,128)(2,1)S(1)} %slice.4.own_ref), channel_id=1, source_target_pairs={{0,1},{1,0},{2,3},{3,2},{4,5},{5,4},{6,7},{7,6},{8,9},{9,8},{10,11... | collective-permute-start | bytes 1179656 | tf_op jit(solution)/shard_map/ppermute | solution.py:400

commit v7 on v6

--- a/solution.py
+++ b/solution.py
@@ -278,8 +278,24 @@
         ].astype(jnp.bfloat16)
 
 
+def place_taps(group, side, part_ref, taps_ref, scr, taps_buf, sem):
+    tokens, channels = taps_ref.shape
+    half = tokens // LANES // 2
+    size = group * half
+    for source in range(part_ref.shape[0]):
+        scr[source * size : (source + 1) * size, :] = part_ref[source].astype(jnp.float32)
+    for row in range(half):
+        span = pl.ds(row * LANES, LANES)
+        taps_buf[span, :] = scr[pl.ds(row, channels, stride=half), :].T.astype(jnp.bfloat16)
+    goal = pl.ds(pl.multiple_of(side * (half * LANES), half * LANES), half * LANES)
+    copy = pltpu.make_async_copy(taps_buf, taps_ref.at[goal, :], sem)
+    copy.start()
+    return copy
+
+
 def unpack_kernel(
-    group, mask_ref, recv_ref, conv_ref, grad_ref, pair_scr, conv_buf, grad_buf, sems
+    group, mask_ref, recv_ref, conv_ref, grad_ref, taps_ref, pair_scr, conv_buf, grad_buf,
+    tap_scr, taps_buf, sems, tap_sem,
 ):
     tokens, channels = conv_ref.shape[1:]
     rows = tokens // LANES
@@ -310,36 +326,20 @@
             )
         )
         copies[-1].start()
+    side = lax.rem(lax.axis_index("dp"), 2)
+    copies.append(
+        place_taps(
+            group, side, recv_ref.at[:, pl.ds(size, group * rows // 2), :], taps_ref,
+            tap_scr, taps_buf, tap_sem,
+        )
+    )
     for copy in copies:
         copy.wait()
 
 
-def unpack_taps_kernel(group, own_ref, other_ref, taps_ref, scr, taps_buf, sems):
-    tokens, channels = taps_ref.shape
-    half = tokens // LANES // 2
-    size = group * half
-    side = lax.rem(lax.axis_index("dp"), 2)
-    copies = []
-    for place, ref in enumerate((own_ref, other_ref)):
-        base = place * ref.shape[0] * size
-        for source in range(ref.shape[0]):
-            scr[base + source * size : base + (source + 1) * size, :] = ref[source].astype(
-                jnp.float32
-            )
-        start = jnp.where(side == place, 0, half * LANES)
-        for row in range(half):
-            slot = place * half + row
-            span = pl.ds(slot * LANES, LANES)
-            taps_buf[span, :] = scr[pl.ds(base + row, channels, stride=half), :].T.astype(
-                jnp.bfloat16
-            )
-            goal = pl.ds(pl.multiple_of(start + row * LANES, LANES), LANES)
-            copies.append(
-                pltpu.make_async_copy(taps_buf.at[span, :], taps_ref.at[goal, :], sems.at[slot])
-            )
-            copies[-1].start()
-    for copy in copies:
-        copy.wait()
+def unpack_taps_kernel(group, other_ref, kept_ref, taps_ref, scr, taps_buf, sem):
+    side = 1 - lax.rem(lax.axis_index("dp"), 2)
+    place_taps(group, side, other_ref, taps_ref, scr, taps_buf, sem).wait()
 
 
 VMEM = pl.BlockSpec(memory_space=pltpu.VMEM)
@@ -398,16 +398,23 @@
     returned = lax.all_to_all(results, everyone, split_axis=0, concat_axis=0, tiled=True, axis_index_groups=ring)
     own_taps = returned[:, group * pair :, :]
     other_taps = lax.ppermute(own_taps, "dp", [(i, i ^ 1) for i in range(replicas)])
-    conv_out, signal_grad = pl.pallas_call(
+    tap_scratch = [
+        pltpu.VMEM(((count * group + 1) * half, LANES), jnp.float32),
+        pltpu.VMEM((half * LANES, channels), jnp.bfloat16),
+    ]
+    conv_out, signal_grad, half_grad = pl.pallas_call(
         functools.partial(unpack_kernel, group),
-        out_shape=[jax.ShapeDtypeStruct(signal.shape, jnp.bfloat16)] * 2,
+        out_shape=[jax.ShapeDtypeStruct(signal.shape, jnp.bfloat16)] * 2
+        + [jax.ShapeDtypeStruct(filter_raw.shape, jnp.bfloat16)],
         in_specs=[SMEM, VMEM],
-        out_specs=[HBM, HBM],
+        out_specs=[HBM, HBM, HBM],
         scratch_shapes=[
             pltpu.VMEM(((count * group + 1) * (pair + PAD), LANES), jnp.float32),
             pltpu.VMEM((tokens, channels), jnp.bfloat16),
             pltpu.VMEM((tokens, channels), jnp.bfloat16),
+            *tap_scratch,
             pltpu.SemaphoreType.DMA((2 * rows,)),
+            pltpu.SemaphoreType.DMA,
         ],
         compiler_params=LIMIT,
         name="unpack",
@@ -415,16 +422,13 @@
     filter_grad = pl.pallas_call(
         functools.partial(unpack_taps_kernel, group),
         out_shape=jax.ShapeDtypeStruct(filter_raw.shape, jnp.bfloat16),
-        in_specs=[VMEM, VMEM],
+        in_specs=[VMEM, HBM],
         out_specs=HBM,
-        scratch_shapes=[
-            pltpu.VMEM(((2 * count * group + 1) * half, LANES), jnp.float32),
-            pltpu.VMEM((tokens, channels), jnp.bfloat16),
-            pltpu.SemaphoreType.DMA((2 * half,)),
-        ],
+        scratch_shapes=[*tap_scratch, pltpu.SemaphoreType.DMA],
+        input_output_aliases={1: 0},
         compiler_params=LIMIT,
         name="unpack_taps",
-    )(own_taps, other_taps)
+    )(other_taps, half_grad)
     return conv_out, signal_grad, filter_grad
 
 

time: 109 us -> 109 us (level)
  transfers between devices with their start and end apart: 1 -> 1, of which waited for: 0 -> 0; matrix products, arithmetic and copies ran while one was open for 0% -> 0% of each run, Pallas kernels for 1% -> 2%
where the time goes in v7:
time: 109 us
  blocking collectives  96.3 us (88%)
  Pallas kernels  9.08 us (8%)
  starting transfers between devices  1.57 us (1%)
  between operations  1.42 us (1%)
    all_to_all x1, blocking collectives, per_device(): lax.all_to_all(results, everyone, split_axis=0, concat_axis=0, tiled=True...  48.5 us
    all_to_all x1, blocking collectives, per_device(): lax.all_to_all(packed, everyone, split_axis=0, concat_axis=0, tiled=True,...  47.8 us
    pallas_call x1, Pallas kernels, per_device(): pl.pallas_call(functools.partial(spectral_kernel, blocks, rows, replicas,...  4.45 us
  transfers between devices with their start and end apart: 1, of which 0 were waited for; matrix products, arithmetic and copies ran while one was open for 0% of the time, Pallas kernels for 2%

profile of v7, /device:TPU:0, one launch (start us, length us, event | category | flops | bytes accessed | tf_op | source)
XLA Modules:
  0.0 108.5 jit_solution(10405346160991326265)
XLA Ops:
  1.3 1.9 %pack.1 = bf16[32,216,128]{2,1,0:T(8,128)(2,1)S(1)} custom-call(s32[1,1]{1,0:T(1,128)S(6)} %copy.17.mask_ref, bf16[1,1024,384]{2,1,0:T(8,128)(2,1)} %signal_ref.1, bf16[1,1024,384]{2,1,0:T(8,128)(2,1)} %grad_ref.1, bf16[1024,384]{1,0:T(8,128)(2,1)} %filter_ref.1), custom_call_target="tpu_custom_call" | custom-call | tf_op jit(solution)/shard_map/pack/pallas_call | solution.py:369
  3.2 0.0 copy-start
  3.2 0.0 copy-start.1
  3.2 0.0 copy-start.2
  3.2 0.0 copy-start.3
  3.2 0.0 copy-start.4
  3.2 0.0 copy-start.5
  3.3 0.0 copy-start.6
  3.3 0.0 copy-start.7
  3.3 47.8 %all_to_all.10.recv_ref = bf16[32,216,128]{2,1,0:T(8,128)(2,1)S(1)} all-to-all(bf16[32,216,128]{2,1,0:T(8,128)(2,1)S(1)} %pack.1), channel_id=1, replica_groups={{0,24,16,8,1,25,17,9,2,26,18,10,3,27,19,11,4,28,20,12,5,29,21,13,6,30,2..., dimensions={0} | all-to-all | bytes 3538944 | tf_op jit(solution)/shard_map/all_to_all | solution.py:385
  51.1 0.0 copy-done
  51.1 0.0 copy-done.1
  51.1 0.0 copy-done.2
  51.1 0.0 copy-done.3
  51.1 0.0 copy-done.4
  51.1 0.0 copy-done.5
  51.2 0.0 copy-done.6
  51.2 0.0 copy-done.7
  51.2 4.4 %spectral.1 = bf16[32,240,128]{2,1,0:T(8,128)(2,1)S(1)} custom-call(bf16[32,216,128]{2,1,0:T(8,128)(2,1)S(1)} %all_to_all.10.recv_ref, bf16[256,128]{1,0:T(8,128)(2,1)S(1)} %copy-done.2, bf16[128,64]{1,0:T(8,128)(2,1)S(1)} %copy-done.4, bf16[256,256]{1,0:T(8,128)(2,1)S(1)} %copy-done, bf16[256,256]{1,0:T(8,128)(2,1)S(1)} %copy-done.1, ...), custom_call_target="tpu_custom_call" | custom-call | tf_op jit(solution)/shard_map/spectral/pallas_call | solution.py:386
  55.6 48.5 %all_to_all.11.recv_ref = bf16[32,240,128]{2,1,0:T(8,128)(2,1)S(1)} all-to-all(bf16[32,240,128]{2,1,0:T(8,128)(2,1)S(1)} %spectral.1), channel_id=1, replica_groups={{0,24,16,8,1,25,17,9,2,26,18,10,3,27,19,11,4,28,20,12,5,29,21,13,6,30,2..., dimensions={0} | all-to-all | bytes 3932160 | tf_op jit(solution)/shard_map/all_to_all | solution.py:398
  104.2 1.6 %collective-permute-start = (bf16[32,48,128]{2,1,0:T(8,128)(2,1)S(1)}, bf16[32,48,128]{2,1,0:T(8,128)(2,1)S(1)}, u32[]{:S(2)}, u32[]{:S(2)}) collective-permute-start(bf16[32,48,128]{2,1,0:T(8,128)(2,1)S(1)} %slice.4), channel_id=1, source_target_pairs={{0,1},{1,0},{2,3},{3,2},{4,5},{5,4},{6,7},{7,6},{8,9},{9,8},{10,11... | collective-permute-start | bytes 1179656 | tf_op jit(solution)/shard_map/ppermute | solution.py:400
  105.8 1.8 %unpack.1 = (bf16[1,1024,384]{2,1,0:T(8,128)(2,1)}, bf16[1,1024,384]{2,1,0:T(8,128)(2,1)}, bf16[1024,384]{1,0:T(8,128)(2,1)}) custom-call(s32[1,1]{1,0:T(1,128)S(6)} %copy.17.mask_ref, bf16[32,240,128]{2,1,0:T(8,128)(2,1)S(1)} %all_to_all.11.recv_ref), custom_call_target="tpu_custom_call" | custom-call | tf_op jit(solution)/shard_map/unpack/pallas_call | solution.py:405
  107.5 0.0 collective-permute-done.other_ref
  107.5 1.0 unpack_taps.1
  (1 shorter events, 0.0 us)
Async XLA Ops:
  3.2 47.9 %copy-start = (bf16[256,256]{1,0:T(8,128)(2,1)S(1)}, bf16[256,256]{1,0:T(8,128)(2,1)}, u32[]{:S(2)}) copy-start(bf16[256,256]{1,0:T(8,128)(2,1)} %constant.18.clone.inner_ref) | copy-start | bytes 393220
  3.2 47.9 %copy-start.1 = (bf16[256,256]{1,0:T(8,128)(2,1)S(1)}, bf16[256,256]{1,0:T(8,128)(2,1)}, u32[]{:S(2)}) copy-start(bf16[256,256]{1,0:T(8,128)(2,1)} %constant.19.clone.inner_back_ref) | copy-start | bytes 393220
  3.2 47.9 %copy-start.2 = (bf16[256,128]{1,0:T(8,128)(2,1)S(1)}, bf16[256,128]{1,0:T(8,128)(2,1)}, u32[]{:S(2)}) copy-start(bf16[256,128]{1,0:T(8,128)(2,1)} %constant.16.clone.first_ref) | copy-start | bytes 196612
  3.2 47.9 %copy-start.3 = (bf16[128,256]{1,0:T(8,128)(2,1)S(1)}, bf16[128,256]{1,0:T(8,128)(2,1)}, u32[]{:S(2)}) copy-start(bf16[128,256]{1,0:T(8,128)(2,1)} %constant.20.clone.last_ref) | copy-start | bytes 196612
  3.2 47.9 %copy-start.4 = (bf16[128,64]{1,0:T(8,128)(2,1)S(1)}, bf16[128,64]{1,0:T(8,128)(2,1)}, u32[]{:S(2)}) copy-start(bf16[128,64]{1,0:T(8,128)(2,1)} %constant.17.clone.first_taps_ref) | copy-start | bytes 49156
  3.2 47.9 %copy-start.5 = (f32[64,128]{1,0:T(8,128)S(1)}, f32[64,128]{1,0:T(8,128)}, u32[]{:S(2)}) copy-start(f32[64,128]{1,0:T(8,128)} %constant.22.clone.twist_cos_ref) | copy-start | bytes 98308
  3.3 47.9 %copy-start.6 = (f32[64,128]{1,0:T(8,128)S(1)}, f32[64,128]{1,0:T(8,128)}, u32[]{:S(2)}) copy-start(f32[64,128]{1,0:T(8,128)} %constant.23.clone.twist_sin_ref) | copy-start | bytes 98308
  3.3 47.9 %copy-start.7 = (bf16[64,128]{1,0:T(8,128)(2,1)S(1)}, bf16[64,128]{1,0:T(8,128)(2,1)}, u32[]{:S(2)}) copy-start(bf16[64,128]{1,0:T(8,128)(2,1)} %constant.21.clone.last_taps_ref) | copy-start | bytes 49156
  104.2 3.3 %collective-permute-start = (bf16[32,48,128]{2,1,0:T(8,128)(2,1)S(1)}, bf16[32,48,128]{2,1,0:T(8,128)(2,1)S(1)}, u32[]{:S(2)}, u32[]{:S(2)}) collective-permute-start(bf16[32,48,128]{2,1,0:T(8,128)(2,1)S(1)} %slice.4), channel_id=1, source_target_pairs={{0,1},{1,0},{2,3},{3,2},{4,5},{5,4},{6,7},{7,6},{8,9},{9,8},{10,11... | collective-permute-start | bytes 1179656 | tf_op jit(solution)/shard_map/ppermute | solution.py:400
